TPU v7x, 32 devices: a whole 2x2x4 slice. The times are simulated.
32 devices in a mesh: groups: 2 (over x), tile: 16 (over z, y, core).
Axes of the slice: x: 2, y: 2, z: 4, core: 2. Of those that a mesh axis runs over, the one named last changes fastest.
Arguments:
- observations: bfloat16 [2048, 64, 256], P(('groups', 'tile')), parts along dimension 0, may hold values from -6 to 6
- pixel_geometry: float32 [2048, 8, 256], P(('groups', 'tile')), parts along dimension 0, as said below
- block_counts: int32 [2048], P(('groups', 'tile')), parts along dimension 0, may hold values from 1 to 256, as said below
- block_tiles: int32 [2048], P(('groups', 'tile')), parts along dimension 0, may hold values from 0 to 511, as said below
- cutoff_lists: int32 [512, 3], replicated, may hold values from 0 to 127, as said below
- patch_geometry: float32 [4, 32768], replicated, as said below
- stress: bfloat16 [64, 65536], P(None, ('groups', 'tile')), parts along dimension 1, may hold values from -3 to 3
- screens: bfloat16 [1024, 64, 256], P(('groups', 'tile')), parts along dimension 0, may hold values from -3 to 3
Outputs:
- stress_gradient: float32 [64, 65536], P(None, ('groups', 'tile')), parts along dimension 1
- screen_gradient: float32 [1024, 64, 256], P(('groups', 'tile')), parts along dimension 0
There are 2 independent parts, one for each index of `groups`. A program takes and returns all parts, laid end to end along the dimension named above; an argument that names none is the same for every part. Nothing has to cross between parts.
Inputs may be any that keep to these rules, and one draw needn't show every extreme that they name: `block_tiles`: the owner of tile t is index t // 32 of tile. Among the 64 blocks of one device at most 8 belong to the tiles of one owner, and some owner gets exactly 8 from every device. The live pixels of a block are its first block_counts pixels. `cutoff_lists`: the 3 entries of a row are different patch blocks. `patch_geometry`: depths are 1 or more; compliances are positive. `pixel_geometry`: u and v lie within 0 to 15; weights are positive.
All inputs are finite; a program needn't handle non-finite values.
Results may differ from a plain program's by a relative error of at most 0.0037.
Values may be sent and summed in bfloat16 or wider, within the bound.
No kernel may reach another device: no remote copies, remote signals or barrier semaphores. Data moves between devices by JAX's collectives and lax.ppermute only.
A program may use at most 128 MiB of HBM per device.

v0:
```python
import functools

import jax
import jax.numpy as jnp
from jax import lax
from jax.experimental import pallas as pl
from jax.experimental.pallas import tpu as pltpu
from jax.sharding import PartitionSpec as P

PBLK = 256
NEAR = 3
SG = 16
CHUNK = 128
LAYER = 4
PAIR = 2
NARROW = 3
ROUNDS = (4, 6, 6)
MIB = 1 << 20
TERMS = 32
CROSS = ((0, 0), (0, 1), (1, 0), (0, 2), (1, 1), (2, 0))


def round_sizes(slots):
    return [slots * r // sum(ROUNDS) for r in ROUNDS]


def pack_kernel(local_tiles, layers, slots, here, tiles, counts, obs_in, pix_in, *rest):
    sizes = round_sizes(slots)
    total = len(sizes)
    obs_out, pix_out = rest[: total * layers], rest[total * layers : (total + 1) * layers]
    obs, pix, obs_all, pix_all, fill, sems = rest[(total + 1) * layers :]
    loads = [
        pltpu.make_async_copy(obs_in, obs, sems.at[0]),
        pltpu.make_async_copy(pix_in, pix, sems.at[1]),
    ]
    for copy in loads:
        copy.start()
    my_layer, my_seat = lax.div(here[0], LAYER), lax.rem(here[0], LAYER)
    chunks = pix.shape[2] // CHUNK
    stride = slots + 1
    for x in range(layers):
        fill[x] = 0
    lane = lax.broadcasted_iota(jnp.int32, (8, CHUNK), 1)
    row = lax.broadcasted_iota(jnp.int32, (8, CHUNK), 0)
    for copy in loads:
        copy.wait()

    def put(b, infos):
        tile = tiles[b]
        count = counts[b]
        owner = lax.div(tile, local_tiles)
        x = lax.div(owner, LAYER) ^ my_layer
        seat = lax.rem(owner, LAYER) ^ my_seat
        spot = lax.rem(seat, PAIR) * PAIR + lax.div(seat, PAIR)
        screen = spot * local_tiles + lax.rem(tile, local_tiles)
        slot = fill[x]
        fill[x] = slot + lax.div(count + CHUNK - 1, CHUNK)
        for c in range(chunks):
            at = slot + c
            live = jnp.clip(count - c * CHUNK, 0, CHUNK)
            obs_all[x * stride + at] = obs[b, :, c * CHUNK : (c + 1) * CHUNK]
            pix_all[x * stride + at] = pix[b, :, c * CHUNK : (c + 1) * CHUNK]
            entry = jnp.where(row == 0, live, jnp.where(row == 1, tile, screen))
            here_only = (lane == at) & (row < 3)
            infos = tuple(
                jnp.where(here_only & (x == i), entry, info) for i, info in enumerate(infos)
            )
        return infos

    infos = lax.fori_loop(
        0, obs.shape[0], put, tuple(jnp.zeros((8, CHUNK), jnp.int32) for _ in range(layers))
    )
    copies = []
    for x in range(layers):
        at = x * stride
        pix_all[at + slots] = infos[x].astype(jnp.float32)
        copies.append((pix_all.at[pl.ds(at, stride)], pix_out[x]))
        for i, size in enumerate(sizes):
            copies.append((obs_all.at[pl.ds(at, size)], obs_out[i * layers + x]))
            at += size
    copies = [pltpu.make_async_copy(a, b, sems.at[i]) for i, (a, b) in enumerate(copies)]
    for copy in copies:
        copy.start()
    for copy in copies:
        copy.wait()


def pack(observations, pixel_geometry, block_counts, block_tiles, here, devices, local_tiles):
    blocks, epochs, width = observations.shape
    layers = devices // LAYER
    slots = LAYER * (2 * blocks // devices) * (width // CHUNK)
    sizes = round_sizes(slots)
    smem = pl.BlockSpec(memory_space=pltpu.SMEM)
    hbm = pl.BlockSpec(memory_space=pl.ANY)
    pix_part = jax.ShapeDtypeStruct((slots + 1, 8, CHUNK), jnp.float32)
    out = pl.pallas_call(
        functools.partial(pack_kernel, local_tiles, layers, slots),
        in_specs=[smem, smem, smem, hbm, hbm],
        out_specs=[hbm] * ((len(sizes) + 1) * layers),
        out_shape=[
            jax.ShapeDtypeStruct((size, epochs, CHUNK), observations.dtype)
            for size in sizes
            for _ in range(layers)
        ]
        + [pix_part] * layers,
        scratch_shapes=[
            pltpu.VMEM(observations.shape, observations.dtype),
            pltpu.VMEM(pixel_geometry.shape, jnp.float32),
            pltpu.VMEM((layers * (slots + 1), epochs, CHUNK), observations.dtype),
            pltpu.VMEM((layers * (slots + 1), 8, CHUNK), jnp.float32),
            pltpu.SMEM((layers,), jnp.int32),
            pltpu.SemaphoreType.DMA(((len(sizes) + 1) * layers,)),
        ],
        compiler_params=pltpu.CompilerParams(vmem_limit_bytes=10 * MIB),
        name="pack",
    )(here, block_tiles, block_counts, observations, pixel_geometry)
    rounds = len(sizes)
    return [out[i * layers : (i + 1) * layers] for i in range(rounds)], out[rounds * layers :]


def split(values):
    parts = []
    for _ in range(3):
        part = lax.reduce_precision(values, 8, 7)
        parts.append(part)
        values = values - part
    return parts


def kernel_split(values):
    parts = []
    for _ in range(3):
        part = values.astype(jnp.bfloat16).astype(jnp.float32)
        parts.append(part)
        values = values - part
    return parts


def fit_kernel(first, final, layers, slots, groups, *refs):
    info, cutoffs, places, spots, origin = refs[:5]
    rest = refs[5:]
    obs_in, pix_in = [], []
    for _ in groups:
        obs_in.append(rest[:layers])
        pix_in.append(rest[layers : 2 * layers])
        rest = rest[2 * layers :]
    patches, forms = rest[:2]
    rest = rest[1:]
    if first:
        screen_parts, stress_parts = rest[1 : 1 + LAYER], rest[1 + LAYER : 1 + 2 * LAYER]
        rest = rest[1 + 2 * LAYER :]
        grad, screen_grad, screens, stress = rest[:4]
        rest = rest[4:]
    else:
        screens, stress = rest[1:3]
        grad, screen_grad = rest[5:7]
        rest = rest[7:]
    outs = rest[:3] if final else ()
    rest = rest[len(outs) :]
    obs, pix = rest[:2]
    buffers = rest[2 : 2 + 15 * PAIR]
    items, sems = rest[2 + 15 * PAIR :]
    sets = [
        [buffers[5 * (PAIR * i + lane) : 5 * (PAIR * i + lane) + 5] for lane in range(PAIR)]
        for i in range(3)
    ]
    epochs = obs.shape[1]
    base = groups[0][0]
    span = sum(size for _, _, size in groups)
    local_tiles = screens.shape[0] // LAYER

    loads = []
    for x in range(layers):
        at = x * span
        for g, (_, low, size) in enumerate(groups):
            loads.append((obs_in[g][x], obs.at[pl.ds(at, size)]))
            loads.append((pix_in[g][x].at[pl.ds(low, size)], pix.at[pl.ds(at, size)]))
            at += size
    if first:
        for parts, whole in ((screen_parts, screens), (stress_parts, stress)):
            size = whole.shape[0] // LAYER
            for i, part in enumerate(parts):
                loads.append((part, whole.at[pl.ds(i * size, size)]))
    loads = [pltpu.make_async_copy(a, b, sems.at[i]) for i, (a, b) in enumerate(loads)]
    for copy in loads:
        copy.start()
    if first:
        grad[...] = jnp.zeros_like(grad)
        screen_grad[...] = jnp.zeros_like(screen_grad)

    def info_of(slot, kind):
        x = lax.div(slot, span)
        return info[(x * 3 + kind) * slots + base + lax.rem(slot, span)]

    def list_slot(slot, total):
        items[total] = slot
        return total + jnp.where(info_of(slot, 0) > 0, 1, 0)

    total = lax.fori_loop(0, layers * span, list_slot, 0)
    for copy in loads:
        copy.wait()

    def item_of(i):
        slot = items[jnp.minimum(i, total - 1)]
        tile = info_of(slot, 1)
        return slot, [cutoffs[tile * NEAR + k] for k in range(NEAR)]

    def spread(i, held):
        rows = pix[item_of(i)[0]]
        columns = rows.T
        for i in range(2):
            held[0][i] = jnp.broadcast_to(columns[:, i : i + 1], (CHUNK, CHUNK))
        le, ln = rows[4:5], rows[5:6]
        along = le * (rows[0:1] - origin[0]) + ln * (rows[1:2] - origin[1])
        row = lax.broadcasted_iota(jnp.int32, (8, CHUNK), 0)
        factors = jnp.where(
            row == 0, along, jnp.where(row == 1, le, jnp.where(row == 2, ln, rows[6:7]))
        )
        parts = kernel_split(factors)
        low = row < 4
        tiles = []
        for first_part, second_part in zip(CROSS[::2], CROSS[1::2]):
            upper = jnp.concatenate([parts[second_part[0]][:4]] * 2, axis=0)
            tiles.append(jnp.where(low, parts[first_part[0]], upper))
        tiles.append(jnp.zeros((8, CHUNK), jnp.float32))
        held[1][...] = jnp.concatenate(tiles, axis=0).T.astype(jnp.bfloat16)

    def make_strips(near, k, begin, end, held, green):
        patch = [
            jnp.broadcast_to(patches[near[k], r : r + 1], (8, PBLK)) for r in range(3)
        ]
        alongs = jnp.dot(
            held[1][begin:end], forms[near[k]], preferred_element_type=jnp.float32
        )
        for low in range(begin, end, 16):
            along = alongs[low - begin : low - begin + 16]
            inverses = []
            for at in (low, low + 8):
                east, north = (
                    jnp.concatenate([held[0][i, at : at + 8]] * (PBLK // CHUNK), axis=1)
                    for i in range(2)
                )
                dx = east - patch[0]
                dy = north - patch[1]
                inverses.append(lax.rsqrt(dx * dx + dy * dy + patch[2]))
            inverse = jnp.concatenate(inverses, axis=0)
            green[low : low + 16, k * PBLK : (k + 1) * PBLK] = (
                along * inverse * inverse * inverse
            ).astype(jnp.bfloat16)

    def make_hats(rows, hats):
        node = lax.broadcasted_iota(jnp.int32, (SG, CHUNK), 0).astype(jnp.float32)
        across = jnp.maximum(0.0, 1.0 - jnp.abs(rows[2:3] - node))
        upward = jnp.maximum(0.0, 1.0 - jnp.abs(rows[3:4] - node))
        for a in range(SG):
            hats[a * SG : (a + 1) * SG] = (across[a : a + 1] * upward).astype(jnp.bfloat16)

    def make_head(i, buffers):
        slot, near = item_of(i)
        make_hats(pix[slot], buffers[1])
        return near

    def predict(i, buffers):
        green, hats = buffers[:2]
        slot, near = item_of(i)
        model = jnp.dot(
            screens[info_of(slot, 2)], hats[...], preferred_element_type=jnp.float32
        )
        for k in range(NEAR):
            model += lax.dot_general(
                stress[pl.ds(pl.multiple_of(spots[near[k]], 16), epochs), :],
                green[:, k * PBLK : (k + 1) * PBLK],
                (((1,), (1,)), ((), ())),
                preferred_element_type=jnp.float32,
            )
        return model

    def weigh(i, model, buffers):
        slot, _ = item_of(i)
        live = jnp.where(i < total, info_of(slot, 0), 0)
        lane = lax.broadcasted_iota(jnp.int32, (1, CHUNK), 1)
        scale = jnp.where(lane < live, pix[slot, 7:8, :], 0.0)
        buffers[2][...] = ((model - obs[slot].astype(jnp.float32)) * scale).astype(jnp.bfloat16)

    def add_patch(near, k, buffers):
        grad[places[near[k]]] += jnp.dot(
            buffers[2][...],
            buffers[0][:, k * PBLK : (k + 1) * PBLK],
            preferred_element_type=jnp.float32,
        )

    def add_screen(slot, buffers):
        screen_grad[info_of(slot, 2)] += lax.dot_general(
            buffers[2][...],
            buffers[1][...],
            (((1,), (1,)), ((), ())),
            preferred_element_type=jnp.float32,
        )

    lanes = range(PAIR)
    half = CHUNK // 2

    def spread_pair(j, buffers):
        for lane in lanes:
            spread(PAIR * j + lane, buffers[lane][3:])

    def make_pair(j, buffers):
        for lane in lanes:
            near = make_head(PAIR * j + lane, buffers[lane])
            for k in range(NEAR):
                for low in (0, half):
                    make_strips(near, k, low, low + half, buffers[lane][3:], buffers[lane][0])

    def model_pair(j, buffers):
        for lane in lanes:
            model = predict(PAIR * j + lane, buffers[lane])
            weigh(PAIR * j + lane, model, buffers[lane])

    def turn(j, using, middle, making):
        now = [item_of(PAIR * j + lane) for lane in lanes]
        coming = [PAIR * (j + 1) + lane for lane in lanes]
        near = [make_head(PAIR * (j + 2) + lane, making[lane]) for lane in lanes]
        models = [predict(coming[lane], middle[lane]) for lane in lanes]

        def strips(k, lane):
            for low in (0, half):
                make_strips(
                    near[lane], k, low, low + half, making[lane][3:], making[lane][0]
                )

        def adds(k):
            for lane in lanes:
                add_patch(now[lane][1], k, using[lane])

        strips(0, 0)
        adds(0)
        spread_pair(j + 3, using)
        strips(0, 1)
        adds(1)
        strips(1, 0)
        for lane in lanes:
            weigh(coming[lane], models[lane], middle[lane])
        strips(1, 1)
        adds(2)
        strips(2, 0)
        for lane in lanes:
            add_screen(now[lane][0], using[lane])
        strips(2, 1)

    @pl.when(total > 0)
    def _():
        pairs = lax.div(total + PAIR - 1, PAIR)
        for j in range(3):
            spread_pair(j, sets[j])
        make_pair(0, sets[0])
        make_pair(1, sets[1])
        model_pair(0, sets[0])

        def step(i, _):
            for at in range(3):
                j = 3 * i + at

                @pl.when(j < pairs)
                def _():
                    turn(j, sets[at], sets[(at + 1) % 3], sets[(at + 2) % 3])

            return 0

        lax.fori_loop(0, lax.div(pairs + 2, 3), step, 0)

    if final:
        half = grad.shape[0] // 2
        outs[0][...] = grad[half:].astype(outs[0].dtype)
        for i, out in enumerate(outs[1:]):
            low = (PAIR + i) * local_tiles
            out[...] = screen_grad[low : low + local_tiles].astype(out.dtype)


def fit(tables, groups, patches, forms, screens, stress, state, first, final):
    layers = len(groups[0][1])
    slots = tables[0].shape[0] // (3 * layers)
    smem = pl.BlockSpec(memory_space=pltpu.SMEM)
    vmem = pl.BlockSpec(memory_space=pltpu.VMEM)
    hbm = pl.BlockSpec(memory_space=pl.ANY)
    spans = tuple((base, low, obs[0].shape[0]) for base, obs, _, low in groups)
    arrays = [a for _, obs, pix, _ in groups for a in (*obs, *pix)]
    span = sum(size for _, _, size in spans)
    blocks, epochs = state[0].shape[0], state[0].shape[1]
    out_shape = [jax.ShapeDtypeStruct(a.shape, a.dtype) for a in state]
    if first:
        state = ()
        for parts in (screens, stress):
            shape = (LAYER * parts[0].shape[0],) + parts[0].shape[1:]
            out_shape.append(jax.ShapeDtypeStruct(shape, parts[0].dtype))
    else:
        screens, stress = [screens], [stress]
    if final:
        out_shape.append(jax.ShapeDtypeStruct((blocks // 2, epochs, PBLK), jnp.bfloat16))
        shape = (state[1].shape[0] // LAYER,) + state[1].shape[1:]
        out_shape += [jax.ShapeDtypeStruct(shape, jnp.bfloat16)] * 2
    before = len(tables) + len(arrays) + 2 + len(screens) + len(stress)
    return pl.pallas_call(
        functools.partial(fit_kernel, first, final, layers, slots, spans),
        in_specs=[smem] * len(tables)
        + [hbm] * len(arrays)
        + [vmem] * 2
        + [hbm if first else vmem] * (len(screens) + len(stress))
        + [vmem] * len(state),
        out_specs=[vmem] * len(out_shape),
        out_shape=out_shape,
        scratch_shapes=[
            pltpu.VMEM((layers * span, epochs, CHUNK), arrays[0].dtype),
            pltpu.VMEM((layers * span, 8, CHUNK), jnp.float32),
        ]
        + [
            pltpu.VMEM((CHUNK, NEAR * PBLK), jnp.bfloat16),
            pltpu.VMEM((SG * SG, CHUNK), jnp.bfloat16),
            pltpu.VMEM((epochs, CHUNK), jnp.bfloat16),
            pltpu.VMEM((2, CHUNK, CHUNK), jnp.float32),
            pltpu.VMEM((CHUNK, TERMS), jnp.bfloat16),
        ]
        * (3 * PAIR)
        + [
            pltpu.SMEM((layers * span + 1,), jnp.int32),
            pltpu.SemaphoreType.DMA((2 * layers * len(groups) + 2 * LAYER,)),
        ],
        input_output_aliases={} if first else {before: 0, before + 1: 1},
        compiler_params=pltpu.CompilerParams(vmem_limit_bytes=8 * MIB),
        cost_estimate=pl.CostEstimate(
            flops=layers * span * 4 * epochs * CHUNK * (NEAR + 1) * PBLK,
            bytes_accessed=1024,
            transcendentals=layers * span * CHUNK * NEAR * PBLK,
        ),
        name="fit",
    )(*tables, *arrays, patches, forms, *screens, *stress, *state)


def partner(values, devices, distance):
    return lax.ppermute(values, "tile", [(i, i ^ distance) for i in range(devices)])


def orders(devices):
    stages = devices.bit_length() - 1
    high = list(range(2, stages))
    return [1] + high, high + [1]


def block_places(devices, here, blocks, local, epochs):
    block = jnp.arange(blocks)
    other = (block // local) ^ here
    seat = block % local
    half = local // 2
    turned = []
    for order in orders(devices):
        spot = 0
        for bit in order:
            spot = spot * 2 + ((other >> bit) & 1)
        turned.append(spot)
    chips = devices // 2
    upper = seat // half
    spot = jnp.where(upper == 0, turned[0], turned[1])
    place = (((other & 1) * 2 + upper) * chips + spot) * half + seat % half
    stages = devices.bit_length() - 1
    held = sum(((other >> (stages - 1 - s)) & 1) << s for s in range(stages))
    return place.astype(jnp.int32), ((held * local + seat) * epochs).astype(jnp.int32)


def halve(kept, given, there, devices):
    total = kept + partner(given, devices, 1).astype(jnp.float32)
    middle = total.shape[0] // 2
    parts = [total[:middle], total[middle:]]
    both = orders(devices)
    stages = len(both[0])
    back = None
    for stage in range(stages):
        got = []
        for side in range(2):
            given = parts[side][parts[side].shape[0] // 2 :]
            if stages - stage <= NARROW:
                given = given.astype(jnp.bfloat16)
            got.append(partner(given, devices, 1 << both[side][stage]))
        for side in range(2):
            if side:
                _, got[1] = lax.optimization_barrier((parts[0], got[1]))
            size = parts[side].shape[0] // 2
            parts[side] = parts[side][:size] + got[side].astype(jnp.float32)
            if back is None:
                _, there = lax.optimization_barrier((parts[0], there))
                back = partner(there, devices, PAIR)
    return jnp.concatenate(parts, axis=0), back


def on_device(
    observations,
    pixel_geometry,
    block_counts,
    block_tiles,
    cutoff_lists,
    patch_geometry,
    stress,
    screens,
):
    devices = lax.axis_size("tile")
    here = lax.axis_index("tile")
    blocks, epochs, width = observations.shape
    local_tiles = screens.shape[0]
    layers = devices // LAYER
    local = stress.shape[1] // PBLK

    slots = LAYER * (2 * blocks // devices) * (width // CHUNK)
    sizes = round_sizes(slots)

    held = jnp.swapaxes(stress.reshape(epochs, local, PBLK), 0, 1).reshape(-1, PBLK)
    other = partner(held, devices, devices // 2)
    across_screens = partner(screens, devices, PAIR)
    obs, pix = pack(
        observations,
        pixel_geometry,
        block_counts,
        block_tiles,
        jnp.reshape(here, (1,)).astype(jnp.int32),
        devices,
        local_tiles,
    )

    def exchange(parts):
        got = [partner(parts[x], devices, x * LAYER) for x in range(layers - 1, 0, -1)]
        return [parts[0]] + got[::-1]

    distance = devices // 2
    while distance >= LAYER:
        if distance < devices // 2:
            other = partner(held, devices, distance)
        held = jnp.concatenate([held, other], axis=0)
        if distance == devices // 2:
            _, pix = lax.optimization_barrier((held, pix))
            pix = exchange(pix)
        distance //= 2
    patch_blocks = devices * local
    east, north, depth, compliance = patch_geometry
    origin = patch_geometry[:2, 0]
    strength = compliance * depth * depth
    faces = split(
        jnp.stack(
            [
                strength,
                -strength * (east - origin[0]),
                -strength * (north - origin[1]),
                strength * depth,
            ]
        )
    )
    forms = jnp.concatenate(
        [faces[second] for _, second in CROSS] + [jnp.zeros((8,) + east.shape, jnp.float32)]
    ).astype(jnp.bfloat16)
    forms = jnp.swapaxes(forms.reshape(TERMS, patch_blocks, PBLK), 0, 1)
    patches = jnp.stack([east, north, depth * depth])
    patches = jnp.swapaxes(patches.reshape(3, patch_blocks, PBLK), 0, 1)
    cutoffs = cutoff_lists.reshape(-1)
    held, pix, across_screens = lax.optimization_barrier((held, pix, across_screens))
    places, spots = block_places(devices, here, patch_blocks, local, epochs)
    info = jnp.stack([p[slots, :3, :slots] for p in pix]).astype(jnp.int32).reshape(-1)
    across_screens, forms, patches, cutoffs, info, places, spots = lax.optimization_barrier(
        (across_screens, forms, patches, cutoffs, info, places, spots)
    )
    got = [exchange(o) for o in obs]
    across = partner(held, devices, PAIR)
    across, got[0] = lax.optimization_barrier((across, got[0]))
    all_stress = [held, across, partner(held, devices, 1), partner(across, devices, 1)]
    all_screens = [
        screens,
        across_screens,
        partner(screens, devices, 1),
        partner(across_screens, devices, 1),
    ]

    tables = (info, cutoffs, places, spots, origin)

    state = (
        jax.ShapeDtypeStruct((patch_blocks, epochs, PBLK), jnp.float32),
        jax.ShapeDtypeStruct((LAYER * local_tiles,) + screens.shape[1:], jnp.float32),
    )
    base = 0
    for i, size in enumerate(sizes):
        first, final = i == 0, i == len(sizes) - 1
        groups = [(base, got[i], pix, base)]
        state = fit(
            tables,
            groups,
            patches,
            forms,
            all_screens,
            all_stress,
            state[:2],
            first,
            final,
        )
        if first:
            all_screens, all_stress = state[2:]
        base += size
    grad, screen_grad, given, next_door, diagonal = state
    own, far = screen_grad[:local_tiles], screen_grad[local_tiles : PAIR * local_tiles]
    there = (far + partner(diagonal, devices, 1).astype(jnp.float32)).astype(jnp.bfloat16)
    grad, back = halve(grad[: grad.shape[0] // 2], given, there, devices)
    screen_gradient = (
        own + partner(next_door, devices, 1).astype(jnp.float32) + back.astype(jnp.float32)
    )
    return (jnp.swapaxes(grad, 0, 1).reshape(epochs, local * PBLK), screen_gradient)


def solution(mesh):
    return jax.shard_map(
        on_device,
        mesh=mesh,
        in_specs=(
            P(("groups", "tile"), None, None),
            P(("groups", "tile"), None, None),
            P(("groups", "tile")),
            P(("groups", "tile")),
            P(),
            P(),
            P(None, ("groups", "tile")),
            P(("groups", "tile"), None, None),
        ),
        out_specs=(P(None, ("groups", "tile")), P(("groups", "tile"), None, None)),
        check_vma=False,
    )
```

profile of v0, /device:TPU:0, one launch (start us, length us, event | category | flops | bytes accessed | tf_op | source)
XLA Modules:
  0.0 219.2 jit_solution(15417174592420931817)
XLA Ops:
  1.7 4.1 %collective-permute-start = (bf16[512,256]{1,0:T(8,128)(2,1)S(1)}, bf16[512,256]{1,0:T(8,128)(2,1)S(1)}, u32[]{:S(2)}, u32[]{:S(2)}) collective-permute-start(bf16[512,256]{1,0:T(8,128)(2,1)S(1)} %bitcast.26), channel_id=1, source_target_pairs={{0,8},{1,9},{2,10},{3,11},{4,12},{5,13},{6,14},{7,15},{8,0},{9,1},... | collective-permute-start | bytes 786440 | tf_op jit(solution)/shard_map/ppermute | solution.py:439
  11.2 5.0 %pack.1 = (bf16[16,64,128]{2,1,0:T(8,128)(2,1)S(1)}, bf16[16,64,128]{2,1,0:T(8,128)(2,1)}, bf16[16,64,128]{2,1,0:T(8,128)(2,1)}, bf16[16,64,128]{2,1,0:T(8,128)(...) custom-call(s32[1]{0:T(128)} %bitcast.3.here, ...), custom_call_target="tpu_custom_call" | custom-call | tf_op jit(solution)/shard_map/pack/pallas_call | solution.py:96
  21.4 1.6 collective-permute-start.1
  23.8 3.6 %collective-permute-start.4 = (f32[65,8,128]{2,1,0:T(8,128)S(1)}, f32[65,8,128]{2,1,0:T(8,128)S(1)}, u32[]{:S(2)}, u32[]{:S(2)}) collective-permute-start(f32[65,8,128]{2,1,0:T(8,128)S(1)} %get-tuple-element.62), channel_id=1, source_target_pairs={{0,12},{1,13},{2,14},{3,15},{4,8},{5,9},{6,10},{7,11},{8,4},{9,5},... | collective-permute-start | bytes 798728 | tf_op jit(solution)/shard_map/ppermute | solution.py:439
  28.4 13.6 %collective-permute-done.1 = bf16[1024,256]{1,0:T(8,128)(2,1)S(1)} collective-permute-done((bf16[1024,256]{1,0:T(8,128)(2,1)S(1)}, bf16[1024,256]{1,0:T(8,128)(2,1)S(1)}, u32[]{:S(2)}, u32[]{:S(2)}) %collective-permute-start.1) | collective-permute-done | bytes 524320 | tf_op jit(solution)/shard_map/ppermute | solution.py:439
  43.1 11.6 %collective-permute-done.2.refs_10_ = f32[65,8,128]{2,1,0:T(8,128)S(1)} collective-permute-done((f32[65,8,128]{2,1,0:T(8,128)S(1)}, f32[65,8,128]{2,1,0:T(8,128)S(1)}, u32[]{:S(2)}, u32[]{:S(2)}) %collective-permute-start.2) | collective-permute-done | bytes 266272 | tf_op jit(solution)/shard_map/ppermute | solution.py:439
  54.7 4.4 %collective-permute-start.12 = (bf16[16,64,128]{2,1,0:T(8,128)(2,1)}, bf16[16,64,128]{2,1,0:T(8,128)(2,1)}, u32[]{:S(2)}, u32[]{:S(2)}) collective-permute-start(bf16[16,64,128]{2,1,0:T(8,128)(2,1)} %get-tuple-element.82), channel_id=1, source_target_pairs={{0,12},{1,13},{2,14},{3,15},{4,8},{5,9},{6,10},{7,11},{8,4},{9,5},... | collective-permute-start | bytes 786440 | tf_op jit(solution)/shard_map/ppermute | solution.py:439
  63.5 8.0 %concatenate.21 = bf16[32,128,256]{2,0,1:T(8,128)(2,1)S(1)} concatenate(bf16[4,128,256]{2,0,1:T(4,128)(2,1)} %get-tuple-element.119, bf16[4,128,256]{2,0,1:T(4,128)(2,1)} %get-tuple-element.118, bf16[4,128,256]{2,0,1:T(4,128)(2,1)} %get-tuple-element.119, bf16[4,128,256]{2,0,1:T(4,128)(2,1)} %get-tuple-element.117, bf16[4,128,256]{2,0,1:T(4,128)(2,1)} %get-tuple-element.118, ...), dimensions={0} | concatenate | bytes 4194304 | tf_op jit(solution)/shard_map/concatenate | solution.py:553
  72.8 5.7 %collective-permute-done.9.refs_20_ = bf16[2048,256]{1,0:T(8,128)(2,1)} collective-permute-done((bf16[2048,256]{1,0:T(8,128)(2,1)}, bf16[2048,256]{1,0:T(8,128)(2,1)}, u32[]{:S(2)}, u32[]{:S(2)}) %collective-permute-start.9) | collective-permute-done | bytes 1048608 | tf_op jit(solution)/shard_map/ppermute | solution.py:439
  78.5 11.7 %collective-permute-done.17.refs_6_ = bf16[24,64,128]{2,1,0:T(8,128)(2,1)S(1)} collective-permute-done((bf16[24,64,128]{2,1,0:T(8,128)(2,1)}, bf16[24,64,128]{2,1,0:T(8,128)(2,1)S(1)}, u32[]{:S(2)}, u32[]{:S(2)}) %collective-permute-start.17) | collective-permute-done | bytes 393248 | tf_op jit(solution)/shard_map/ppermute | solution.py:439
  90.3 2.6 %collective-permute-start.19 = (bf16[24,64,128]{2,1,0:T(8,128)(2,1)}, bf16[24,64,128]{2,1,0:T(8,128)(2,1)S(1)}, u32[]{:S(2)}, u32[]{:S(2)}) collective-permute-start(bf16[24,64,128]{2,1,0:T(8,128)(2,1)} %copy-done.21), channel_id=1, source_target_pairs={{0,12},{1,13},{2,14},{3,15},{4,8},{5,9},{6,10},{7,11},{8,4},{9,5},... | collective-permute-start | bytes 1179656 | tf_op jit(solution)/shard_map/ppermute | solution.py:439
  95.5 2.6 %collective-permute-start.8 = (bf16[24,64,128]{2,1,0:T(8,128)(2,1)}, bf16[24,64,128]{2,1,0:T(8,128)(2,1)S(1)}, u32[]{:S(2)}, u32[]{:S(2)}) collective-permute-start(bf16[24,64,128]{2,1,0:T(8,128)(2,1)} %copy-done.18), channel_id=1, source_target_pairs={{0,12},{1,13},{2,14},{3,15},{4,8},{5,9},{6,10},{7,11},{8,4},{9,5},... | collective-permute-start | bytes 1179656 | tf_op jit(solution)/shard_map/ppermute | solution.py:439
  101.3 23.5 %fit.3 = (f32[128,64,256]{2,1,0:T(8,128)S(1)}, f32[128,64,256]{2,1,0:T(8,128)S(1)}, bf16[128,64,256]{2,1,0:T(8,128)(2,1)S(1)}, bf16[8192,256]{1,0:T(8,128)(2,1)S(1)}) custom-call(s32[768]{0:T(1024)S(1)} %convert_element_type.49.refs_0_, s32[1536]{0:T(1024)S(1)} %reshape.52.refs_1_, s32[128]{0:T(128)S(1)} %get-tuple-element.70.refs_2_, ...), custom_call_target="tpu_custom_call" | custom-call | flops 2147483648 | bytes 1024 | tf_op jit(solution)/shard_map/fit/pallas_call | solution.py:402
  124.9 28.3 %fit.4 = (f32[128,64,256]{2,1,0:T(8,128)S(1)}, f32[128,64,256]{2,1,0:T(8,128)S(1)}) custom-call(s32[768]{0:T(1024)S(1)} %convert_element_type.49.refs_0_, s32[1536]{0:T(1024)S(1)} %reshape.52.refs_1_, s32[128]{0:T(128)S(1)} %get-tuple-element.70.refs_2_, s32[128]{0:T(128)S(1)} %get-tuple-element.71.refs_3_, ...), custom_call_target="tpu_custom_call", output_to_operand_aliasing={{0}: (17, {}), {1}: (18, {})} | custom-call | flops 3221225472 | bytes 1024 | tf_op jit(solution)/shard_map/fit/pallas_call | solution.py:402
  153.2 4.3 %fit.5 = (f32[128,64,256]{2,1,0:T(8,128)S(1)}, f32[128,64,256]{2,1,0:T(8,128)S(1)}, bf16[64,64,256]{2,1,0:T(8,128)(2,1)S(1)}, bf16[32,64,256]{2,1,0:T(8,128)(2,1)S(1)}, bf16[32,64,256]{2,1,0:T(8,128)(2,1)S(1)}) custom-call(s32[768]{0:T(1024)S(1)} %convert_element_type.49.refs_0_, ...), custom_call_target="tpu_custom_call", output_to_operand_aliasing={{0}: (17, {}), {1}: (18, {})} | custom-call | flops 3221225472 | bytes 1024 | tf_op jit(solution)/shard_map/fit/pallas_call | solution.py:402
  159.5 4.2 %collective-permute-done.20 = bf16[64,64,256]{2,1,0:T(8,128)(2,1)S(1)} collective-permute-done((bf16[64,64,256]{2,1,0:T(8,128)(2,1)S(1)}, bf16[64,64,256]{2,1,0:T(8,128)(2,1)S(1)}, u32[]{:S(2)}, u32[]{:S(2)}) %collective-permute-start.20) | collective-permute-done | bytes 2097184 | tf_op jit(solution)/shard_map/ppermute | solution.py:439
  166.1 8.4 %collective-permute-start.24 = (bf16[16,64,256]{2,1,0:T(8,128)(2,1)S(1)}, bf16[16,64,256]{2,1,0:T(8,128)(2,1)S(1)}, u32[]{:S(2)}, u32[]{:S(2)}) collective-permute-start(bf16[16,64,256]{2,1,0:T(8,128)(2,1)S(1)} %get-tuple-element.112), channel_id=1, source_target_pairs={{0,4},{1,5},{2,6},{3,7},{4,0},{5,1},{6,2},{7,3},{8,12},{9,13},{10,... | collective-permute-start | bytes 1572872 | tf_op jit(solution)/shard_map/ppermute | solution.py:439
  174.6 4.3 %collective-permute-done.21 = bf16[16,64,256]{2,1,0:T(8,128)(2,1)S(1)} collective-permute-done((bf16[16,64,256]{2,1,0:T(8,128)(2,1)S(1)}, bf16[16,64,256]{2,1,0:T(8,128)(2,1)S(1)}, u32[]{:S(2)}, u32[]{:S(2)}) %collective-permute-start.21) | collective-permute-done | bytes 524320 | tf_op jit(solution)/shard_map/ppermute | solution.py:439
  179.0 7.9 %collective-permute-done.24 = bf16[16,64,256]{2,1,0:T(8,128)(2,1)S(1)} collective-permute-done((bf16[16,64,256]{2,1,0:T(8,128)(2,1)S(1)}, bf16[16,64,256]{2,1,0:T(8,128)(2,1)S(1)}, u32[]{:S(2)}, u32[]{:S(2)}) %collective-permute-start.24) | collective-permute-done | bytes 524320 | tf_op jit(solution)/shard_map/ppermute | solution.py:439
  187.1 1.8 collective-permute-start.22
  190.3 8.4 %collective-permute-done.22 = bf16[8,64,256]{2,1,0:T(8,128)(2,1)S(1)} collective-permute-done((bf16[8,64,256]{2,1,0:T(8,128)(2,1)S(1)}, bf16[8,64,256]{2,1,0:T(8,128)(2,1)S(1)}, u32[]{:S(2)}, u32[]{:S(2)}) %collective-permute-start.22) | collective-permute-done | bytes 262176 | tf_op jit(solution)/shard_map/ppermute | solution.py:439
  199.6 7.6 %collective-permute-done.25 = bf16[8,64,256]{2,1,0:T(8,128)(2,1)S(1)} collective-permute-done((bf16[8,64,256]{2,1,0:T(8,128)(2,1)S(1)}, bf16[8,64,256]{2,1,0:T(8,128)(2,1)S(1)}, u32[]{:S(2)}, u32[]{:S(2)}) %collective-permute-start.25) | collective-permute-done | bytes 262176 | tf_op jit(solution)/shard_map/ppermute | solution.py:439
  208.6 7.9 %collective-permute-done.26 = bf16[4,64,256]{2,1,0:T(8,128)(2,1)S(1)} collective-permute-done((bf16[4,64,256]{2,1,0:T(8,128)(2,1)S(1)}, bf16[4,64,256]{2,1,0:T(8,128)(2,1)S(1)}, u32[]{:S(2)}, u32[]{:S(2)}) %collective-permute-start.26) | collective-permute-done | bytes 131104 | tf_op jit(solution)/shard_map/ppermute | solution.py:439
  217.4 1.8 convert_add_fusion.1
  (130 shorter events, 35.2 us)
Async XLA Ops:
  1.7 19.7 %collective-permute-start = (bf16[512,256]{1,0:T(8,128)(2,1)S(1)}, bf16[512,256]{1,0:T(8,128)(2,1)S(1)}, u32[]{:S(2)}, u32[]{:S(2)}) collective-permute-start(bf16[512,256]{1,0:T(8,128)(2,1)S(1)} %bitcast.26), channel_id=1, source_target_pairs={{0,8},{1,9},{2,10},{3,11},{4,12},{5,13},{6,14},{7,15},{8,0},{9,1},... | collective-permute-start | bytes 786440 | tf_op jit(solution)/shard_map/ppermute | solution.py:439
  5.8 53.3 %collective-permute-start.5 = (bf16[32,64,256]{2,1,0:T(8,128)(2,1)}, bf16[32,64,256]{2,1,0:T(8,128)(2,1)S(1)}, u32[]{:S(2)}, u32[]{:S(2)}) collective-permute-start(bf16[32,64,256]{2,1,0:T(8,128)(2,1)} %refs_15_.1), channel_id=1, source_target_pairs={{0,2},{1,3},{2,0},{3,1},{4,6},{5,7},{6,4},{7,5},{8,10},{9,11},{10,... | collective-permute-start | bytes 3145736 | tf_op jit(solution)/shard_map/ppermute | solution.py:439
  21.4 20.6 %collective-permute-start.1 = (bf16[1024,256]{1,0:T(8,128)(2,1)S(1)}, bf16[1024,256]{1,0:T(8,128)(2,1)S(1)}, u32[]{:S(2)}, u32[]{:S(2)}) collective-permute-start(bf16[1024,256]{1,0:T(8,128)(2,1)S(1)} %pad_maximum_fusion.1), channel_id=1, source_target_pairs={{0,4},{1,5},{2,6},{3,7},{4,0},{5,1},{6,2},{7,3},{8,12},{9,13},{10,... | collective-permute-start | bytes 1572872 | tf_op jit(solution)/shard_map/ppermute | solution.py:439
  23.0 31.7 %collective-permute-start.2 = (f32[65,8,128]{2,1,0:T(8,128)S(1)}, f32[65,8,128]{2,1,0:T(8,128)S(1)}, u32[]{:S(2)}, u32[]{:S(2)}) collective-permute-start(f32[65,8,128]{2,1,0:T(8,128)S(1)} %get-tuple-element.60), channel_id=1, source_target_pairs={{0,4},{1,5},{2,6},{3,7},{4,0},{5,1},{6,2},{7,3},{8,12},{9,13},{10,... | collective-permute-start | bytes 798728 | tf_op jit(solution)/shard_map/ppermute | solution.py:439
  23.5 31.2 %collective-permute-start.3 = (f32[65,8,128]{2,1,0:T(8,128)S(1)}, f32[65,8,128]{2,1,0:T(8,128)S(1)}, u32[]{:S(2)}, u32[]{:S(2)}) collective-permute-start(f32[65,8,128]{2,1,0:T(8,128)S(1)} %get-tuple-element.61), channel_id=1, source_target_pairs={{0,8},{1,9},{2,10},{3,11},{4,12},{5,13},{6,14},{7,15},{8,0},{9,1},... | collective-permute-start | bytes 798728 | tf_op jit(solution)/shard_map/ppermute | solution.py:439
  23.8 30.9 %collective-permute-start.4 = (f32[65,8,128]{2,1,0:T(8,128)S(1)}, f32[65,8,128]{2,1,0:T(8,128)S(1)}, u32[]{:S(2)}, u32[]{:S(2)}) collective-permute-start(f32[65,8,128]{2,1,0:T(8,128)S(1)} %get-tuple-element.62), channel_id=1, source_target_pairs={{0,12},{1,13},{2,14},{3,15},{4,8},{5,9},{6,10},{7,11},{8,4},{9,5},... | collective-permute-start | bytes 798728 | tf_op jit(solution)/shard_map/ppermute | solution.py:439
  42.0 48.3 %collective-permute-start.13 = (bf16[32,64,256]{2,1,0:T(8,128)(2,1)}, bf16[32,64,256]{2,1,0:T(8,128)(2,1)}, u32[]{:S(2)}, u32[]{:S(2)}) collective-permute-start(bf16[32,64,256]{2,1,0:T(8,128)(2,1)} %refs_15_.1), channel_id=1, source_target_pairs={{0,1},{1,0},{2,3},{3,2},{4,5},{5,4},{6,7},{7,6},{8,9},{9,8},{10,11... | collective-permute-start | bytes 3145736 | tf_op jit(solution)/shard_map/ppermute | solution.py:439
  54.7 17.6 %collective-permute-start.10 = (bf16[16,64,128]{2,1,0:T(8,128)(2,1)}, bf16[16,64,128]{2,1,0:T(8,128)(2,1)}, u32[]{:S(2)}, u32[]{:S(2)}) collective-permute-start(bf16[16,64,128]{2,1,0:T(8,128)(2,1)} %get-tuple-element.80), channel_id=1, source_target_pairs={{0,4},{1,5},{2,6},{3,7},{4,0},{5,1},{6,2},{7,3},{8,12},{9,13},{10,... | collective-permute-start | bytes 786440 | tf_op jit(solution)/shard_map/ppermute | solution.py:439
  54.7 17.6 %collective-permute-start.11 = (bf16[16,64,128]{2,1,0:T(8,128)(2,1)}, bf16[16,64,128]{2,1,0:T(8,128)(2,1)}, u32[]{:S(2)}, u32[]{:S(2)}) collective-permute-start(bf16[16,64,128]{2,1,0:T(8,128)(2,1)} %get-tuple-element.81), channel_id=1, source_target_pairs={{0,8},{1,9},{2,10},{3,11},{4,12},{5,13},{6,14},{7,15},{8,0},{9,1},... | collective-permute-start | bytes 786440 | tf_op jit(solution)/shard_map/ppermute | solution.py:439
  54.7 18.1 %collective-permute-start.12 = (bf16[16,64,128]{2,1,0:T(8,128)(2,1)}, bf16[16,64,128]{2,1,0:T(8,128)(2,1)}, u32[]{:S(2)}, u32[]{:S(2)}) collective-permute-start(bf16[16,64,128]{2,1,0:T(8,128)(2,1)} %get-tuple-element.82), channel_id=1, source_target_pairs={{0,12},{1,13},{2,14},{3,15},{4,8},{5,9},{6,10},{7,11},{8,4},{9,5},... | collective-permute-start | bytes 786440 | tf_op jit(solution)/shard_map/ppermute | solution.py:439
  59.1 19.4 %collective-permute-start.9 = (bf16[2048,256]{1,0:T(8,128)(2,1)}, bf16[2048,256]{1,0:T(8,128)(2,1)}, u32[]{:S(2)}, u32[]{:S(2)}) collective-permute-start(bf16[2048,256]{1,0:T(8,128)(2,1)} %pad_maximum_fusion.refs_19_), channel_id=1, source_target_pairs={{0,2},{1,3},{2,0},{3,1},{4,6},{5,7},{6,4},{7,5},{8,10},{9,11},{10,... | collective-permute-start | bytes 3145736 | tf_op jit(solution)/shard_map/ppermute | solution.py:439
  72.3 22.3 %collective-permute-start.15 = (bf16[2048,256]{1,0:T(8,128)(2,1)}, bf16[2048,256]{1,0:T(8,128)(2,1)S(1)}, u32[]{:S(2)}, u32[]{:S(2)}) collective-permute-start(bf16[2048,256]{1,0:T(8,128)(2,1)} %pad_maximum_fusion.refs_19_), channel_id=1, source_target_pairs={{0,1},{1,0},{2,3},{3,2},{4,5},{5,4},{6,7},{7,6},{8,9},{9,8},{10,11... | collective-permute-start | bytes 3145736 | tf_op jit(solution)/shard_map/ppermute | solution.py:439
  72.3 21.4 %collective-permute-start.14 = (bf16[32,64,256]{2,1,0:T(8,128)(2,1)}, bf16[32,64,256]{2,1,0:T(8,128)(2,1)S(1)}, u32[]{:S(2)}, u32[]{:S(2)}) collective-permute-start(bf16[32,64,256]{2,1,0:T(8,128)(2,1)} %copy-done.3), channel_id=1, source_target_pairs={{0,1},{1,0},{2,3},{3,2},{4,5},{5,4},{6,7},{7,6},{8,9},{9,8},{10,11... | collective-permute-start | bytes 3145736 | tf_op jit(solution)/shard_map/ppermute | solution.py:439
  78.5 17.0 %collective-permute-start.16 = (bf16[2048,256]{1,0:T(8,128)(2,1)}, bf16[2048,256]{1,0:T(8,128)(2,1)S(1)}, u32[]{:S(2)}, u32[]{:S(2)}) collective-permute-start(bf16[2048,256]{1,0:T(8,128)(2,1)} %collective-permute-done.9.refs_20_), channel_id=1, source_target_pairs={{0,1},{1,0},{2,3},{3,2},{4,5},{5,4},{6,7},{7,6},{8,9},{9,8},{10,11... | collective-permute-start | bytes 3145736 | tf_op jit(solution)/shard_map/ppermute | solution.py:439
  90.3 34.6 %collective-permute-start.18 = (bf16[24,64,128]{2,1,0:T(8,128)(2,1)}, bf16[24,64,128]{2,1,0:T(8,128)(2,1)S(1)}, u32[]{:S(2)}, u32[]{:S(2)}) collective-permute-start(bf16[24,64,128]{2,1,0:T(8,128)(2,1)} %copy-done.22), channel_id=1, source_target_pairs={{0,8},{1,9},{2,10},{3,11},{4,12},{5,13},{6,14},{7,15},{8,0},{9,1},... | collective-permute-start | bytes 1179656 | tf_op jit(solution)/shard_map/ppermute | solution.py:439
  90.3 34.6 %collective-permute-start.19 = (bf16[24,64,128]{2,1,0:T(8,128)(2,1)}, bf16[24,64,128]{2,1,0:T(8,128)(2,1)S(1)}, u32[]{:S(2)}, u32[]{:S(2)}) collective-permute-start(bf16[24,64,128]{2,1,0:T(8,128)(2,1)} %copy-done.21), channel_id=1, source_target_pairs={{0,12},{1,13},{2,14},{3,15},{4,8},{5,9},{6,10},{7,11},{8,4},{9,5},... | collective-permute-start | bytes 1179656 | tf_op jit(solution)/shard_map/ppermute | solution.py:439
  93.7 59.5 %collective-permute-start.6 = (bf16[24,64,128]{2,1,0:T(8,128)(2,1)}, bf16[24,64,128]{2,1,0:T(8,128)(2,1)S(1)}, u32[]{:S(2)}, u32[]{:S(2)}) collective-permute-start(bf16[24,64,128]{2,1,0:T(8,128)(2,1)} %copy-done.20), channel_id=1, source_target_pairs={{0,4},{1,5},{2,6},{3,7},{4,0},{5,1},{6,2},{7,3},{8,12},{9,13},{10,... | collective-permute-start | bytes 1179656 | tf_op jit(solution)/shard_map/ppermute | solution.py:439
  94.6 58.6 %collective-permute-start.7 = (bf16[24,64,128]{2,1,0:T(8,128)(2,1)}, bf16[24,64,128]{2,1,0:T(8,128)(2,1)S(1)}, u32[]{:S(2)}, u32[]{:S(2)}) collective-permute-start(bf16[24,64,128]{2,1,0:T(8,128)(2,1)} %copy-done.19), channel_id=1, source_target_pairs={{0,8},{1,9},{2,10},{3,11},{4,12},{5,13},{6,14},{7,15},{8,0},{9,1},... | collective-permute-start | bytes 1179656 | tf_op jit(solution)/shard_map/ppermute | solution.py:439
  95.5 57.7 %collective-permute-start.8 = (bf16[24,64,128]{2,1,0:T(8,128)(2,1)}, bf16[24,64,128]{2,1,0:T(8,128)(2,1)S(1)}, u32[]{:S(2)}, u32[]{:S(2)}) collective-permute-start(bf16[24,64,128]{2,1,0:T(8,128)(2,1)} %copy-done.18), channel_id=1, source_target_pairs={{0,12},{1,13},{2,14},{3,15},{4,8},{5,9},{6,10},{7,11},{8,4},{9,5},... | collective-permute-start | bytes 1179656 | tf_op jit(solution)/shard_map/ppermute | solution.py:439
  165.9 23.0 %collective-permute-start.28 = (bf16[32,64,256]{2,1,0:T(8,128)(2,1)S(1)}, bf16[32,64,256]{2,1,0:T(8,128)(2,1)S(1)}, u32[]{:S(2)}, u32[]{:S(2)}) collective-permute-start(bf16[32,64,256]{2,1,0:T(8,128)(2,1)S(1)} %copy-done.17), channel_id=1, source_target_pairs={{0,1},{1,0},{2,3},{3,2},{4,5},{5,4},{6,7},{7,6},{8,9},{9,8},{10,11... | collective-permute-start | bytes 3145736 | tf_op jit(solution)/shard_map/ppermute | solution.py:439
  166.1 20.9 %collective-permute-start.24 = (bf16[16,64,256]{2,1,0:T(8,128)(2,1)S(1)}, bf16[16,64,256]{2,1,0:T(8,128)(2,1)S(1)}, u32[]{:S(2)}, u32[]{:S(2)}) collective-permute-start(bf16[16,64,256]{2,1,0:T(8,128)(2,1)S(1)} %get-tuple-element.112), channel_id=1, source_target_pairs={{0,4},{1,5},{2,6},{3,7},{4,0},{5,1},{6,2},{7,3},{8,12},{9,13},{10,... | collective-permute-start | bytes 1572872 | tf_op jit(solution)/shard_map/ppermute | solution.py:439
  174.5 42.9 %collective-permute-start.27 = (bf16[32,64,256]{2,1,0:T(8,128)(2,1)S(1)}, bf16[32,64,256]{2,1,0:T(8,128)(2,1)S(1)}, u32[]{:S(2)}, u32[]{:S(2)}) collective-permute-start(bf16[32,64,256]{2,1,0:T(8,128)(2,1)S(1)} %copy-done.15), channel_id=1, source_target_pairs={{0,1},{1,0},{2,3},{3,2},{4,5},{5,4},{6,7},{7,6},{8,9},{9,8},{10,11... | collective-permute-start | bytes 3145736 | tf_op jit(solution)/shard_map/ppermute | solution.py:439
  188.9 18.3 %collective-permute-start.25 = (bf16[8,64,256]{2,1,0:T(8,128)(2,1)S(1)}, bf16[8,64,256]{2,1,0:T(8,128)(2,1)S(1)}, u32[]{:S(2)}, u32[]{:S(2)}) collective-permute-start(bf16[8,64,256]{2,1,0:T(8,128)(2,1)S(1)} %slice.131), channel_id=1, source_target_pairs={{0,8},{1,9},{2,10},{3,11},{4,12},{5,13},{6,14},{7,15},{8,0},{9,1},... | collective-permute-start | bytes 786440 | tf_op jit(solution)/shard_map/ppermute | solution.py:439
  189.3 28.1 %collective-permute-start.29 = (bf16[32,64,256]{2,1,0:T(8,128)(2,1)S(1)}, bf16[32,64,256]{2,1,0:T(8,128)(2,1)S(1)}, u32[]{:S(2)}, u32[]{:S(2)}) collective-permute-start(bf16[32,64,256]{2,1,0:T(8,128)(2,1)S(1)} %add_convert_fusion), channel_id=1, source_target_pairs={{0,2},{1,3},{2,0},{3,1},{4,6},{5,7},{6,4},{7,5},{8,10},{9,11},{10,... | collective-permute-start | bytes 3145736 | tf_op jit(solution)/shard_map/ppermute | solution.py:439
  (33 other events, 232.6 us)
where the time goes:
time: 220 us; the launch traced here: 219 us
  waiting for transfers between devices  83.1 us (38%)
  Pallas kernels  61.1 us (28%)
  starting transfers between devices  37.4 us (17%)
  local copies, waits for them, and re-layouts  28 us (13%)
  other arithmetic  8.6 us (4%)
    ppermute x30, waiting for transfers between devices, partner(): lax.ppermute(values, 'tile', [(i, i ^ distance) for i in range(devices)])  83.1 us
    pallas_call x3, Pallas kernels, fit(): pl.pallas_call(functools.partial(fit_kernel, first, final, layers, slots,...  56.1 us
    ppermute x30, starting transfers between devices, partner(): lax.ppermute(values, 'tile', [(i, i ^ distance) for i in range(devices)])  37.4 us
    unnamed x53, local copies, waits for them, and re-layouts  14.8 us
    concatenate x1, local copies, waits for them, and re-layouts, on_device(): jnp.concatenate([faces[second] for _, second in CROSS] + [jnp.zeros((8,)...  8.04 us
    pallas_call x1, Pallas kernels, pack(): pl.pallas_call(functools.partial(pack_kernel, local_tiles, layers, slots)...  4.98 us
  transfers between devices with their start and end apart: 30, of which 11 were waited for; matrix products, arithmetic and copies ran while one was open for 8% of the time, Pallas kernels for 26%

commit v1 on v0

--- a/solution.py
+++ b/solution.py
@@ -563,7 +563,7 @@
     across_screens, forms, patches, cutoffs, info, places, spots = lax.optimization_barrier(
         (across_screens, forms, patches, cutoffs, info, places, spots)
     )
-    got = [exchange(o) for o in obs]
+    got = [exchange(o) for o in obs[:PAIR]]
     across = partner(held, devices, PAIR)
     across, got[0] = lax.optimization_barrier((across, got[0]))
     all_stress = [held, across, partner(held, devices, 1), partner(across, devices, 1)]
@@ -597,6 +597,9 @@
         )
         if first:
             all_screens, all_stress = state[2:]
+            for late in obs[PAIR:]:
+                _, late = lax.optimization_barrier((all_screens, late))
+                got.append(exchange(late))
         base += size
     grad, screen_grad, given, next_door, diagonal = state
     own, far = screen_grad[:local_tiles], screen_grad[local_tiles : PAIR * local_tiles]

time: 220 us -> 213 us (0.968)
  Pallas kernels: 61.1 us -> 47 us
  starting transfers between devices: 37.4 us -> 49.6 us
  waiting for transfers between devices: 83.1 us -> 78.5 us
    pallas_call x3, Pallas kernels: 56.1 us -> 42 us  [fit(): pl.pallas_call(functools.partial(fit_kernel, first, final, layers, slots,...]
    ppermute x30, starting transfers between devices: 37.4 us -> 49.6 us  [partner(): lax.ppermute(values, 'tile', [(i, i ^ distance) for i in range(devices)])]
    ppermute x30, waiting for transfers between devices: 83.1 us -> 78.5 us  [partner(): lax.ppermute(values, 'tile', [(i, i ^ distance) for i in range(devices)])]
    unnamed x53 -> x59, local copies, waits for them, and re-layouts: 14.8 us -> 14.3 us
  transfers between devices with their start and end apart: 30 -> 30, of which waited for: 11 -> 10; matrix products, arithmetic and copies ran while one was open for 8% -> 9% of each run, Pallas kernels for 26% -> 20%
where the time goes in v1:
time: 213 us; the launch traced here: 212 us
  waiting for transfers between devices  78.5 us (37%)
  starting transfers between devices  49.6 us (23%)
  Pallas kernels  47 us (22%)
  local copies, waits for them, and re-layouts  27.6 us (13%)
  other arithmetic  8.62 us (4%)
    ppermute x30, waiting for transfers between devices, partner(): lax.ppermute(values, 'tile', [(i, i ^ distance) for i in range(devices)])  78.5 us
    ppermute x30, starting transfers between devices, partner(): lax.ppermute(values, 'tile', [(i, i ^ distance) for i in range(devices)])  49.6 us
    pallas_call x3, Pallas kernels, fit(): pl.pallas_call(functools.partial(fit_kernel, first, final, layers, slots,...  42 us
    unnamed x59, local copies, waits for them, and re-layouts  14.3 us
    concatenate x1, local copies, waits for them, and re-layouts, on_device(): jnp.concatenate([faces[second] for _, second in CROSS] + [jnp.zeros((8,)...  8.03 us
    pallas_call x1, Pallas kernels, pack(): pl.pallas_call(functools.partial(pack_kernel, local_tiles, layers, slots)...  4.98 us
  transfers between devices with their start and end apart: 30, of which 10 were waited for; matrix products, arithmetic and copies ran while one was open for 9% of the time, Pallas kernels for 20%

profile of v1, /device:TPU:0, one launch (start us, length us, event | category | flops | bytes accessed | tf_op | source)
XLA Modules:
  0.0 212.3 jit_solution(3931673538661821339)
XLA Ops:
  1.7 4.1 %collective-permute-start = (bf16[512,256]{1,0:T(8,128)(2,1)S(1)}, bf16[512,256]{1,0:T(8,128)(2,1)S(1)}, u32[]{:S(2)}, u32[]{:S(2)}) collective-permute-start(bf16[512,256]{1,0:T(8,128)(2,1)S(1)} %bitcast.26), channel_id=1, source_target_pairs={{0,8},{1,9},{2,10},{3,11},{4,12},{5,13},{6,14},{7,15},{8,0},{9,1},... | collective-permute-start | bytes 786440 | tf_op jit(solution)/shard_map/ppermute | solution.py:439
  11.2 5.0 %pack.1 = (bf16[16,64,128]{2,1,0:T(8,128)(2,1)S(1)}, bf16[16,64,128]{2,1,0:T(8,128)(2,1)}, bf16[16,64,128]{2,1,0:T(8,128)(2,1)}, bf16[16,64,128]{2,1,0:T(8,128)(...) custom-call(s32[1]{0:T(128)} %bitcast.3.here, ...), custom_call_target="tpu_custom_call" | custom-call | tf_op jit(solution)/shard_map/pack/pallas_call | solution.py:96
  23.9 3.6 %collective-permute-start.4 = (f32[65,8,128]{2,1,0:T(8,128)S(1)}, f32[65,8,128]{2,1,0:T(8,128)S(1)}, u32[]{:S(2)}, u32[]{:S(2)}) collective-permute-start(f32[65,8,128]{2,1,0:T(8,128)S(1)} %get-tuple-element.66), channel_id=1, source_target_pairs={{0,12},{1,13},{2,14},{3,15},{4,8},{5,9},{6,10},{7,11},{8,4},{9,5},... | collective-permute-start | bytes 798728 | tf_op jit(solution)/shard_map/ppermute | solution.py:439
  28.5 13.6 %collective-permute-done.1 = bf16[1024,256]{1,0:T(8,128)(2,1)S(1)} collective-permute-done((bf16[1024,256]{1,0:T(8,128)(2,1)S(1)}, bf16[1024,256]{1,0:T(8,128)(2,1)S(1)}, u32[]{:S(2)}, u32[]{:S(2)}) %collective-permute-start.1) | collective-permute-done | bytes 524320 | tf_op jit(solution)/shard_map/ppermute | solution.py:439
  43.2 11.6 %collective-permute-done.2.refs_10_ = f32[65,8,128]{2,1,0:T(8,128)S(1)} collective-permute-done((f32[65,8,128]{2,1,0:T(8,128)S(1)}, f32[65,8,128]{2,1,0:T(8,128)S(1)}, u32[]{:S(2)}, u32[]{:S(2)}) %collective-permute-start.2) | collective-permute-done | bytes 266272 | tf_op jit(solution)/shard_map/ppermute | solution.py:439
  54.8 4.4 %collective-permute-start.9 = (bf16[16,64,128]{2,1,0:T(8,128)(2,1)}, bf16[16,64,128]{2,1,0:T(8,128)(2,1)}, u32[]{:S(2)}, u32[]{:S(2)}) collective-permute-start(bf16[16,64,128]{2,1,0:T(8,128)(2,1)} %get-tuple-element.80), channel_id=1, source_target_pairs={{0,12},{1,13},{2,14},{3,15},{4,8},{5,9},{6,10},{7,11},{8,4},{9,5},... | collective-permute-start | bytes 786440 | tf_op jit(solution)/shard_map/ppermute | solution.py:439
  63.7 8.0 %concatenate.21 = bf16[32,128,256]{2,0,1:T(8,128)(2,1)S(1)} concatenate(bf16[4,128,256]{2,0,1:T(4,128)(2,1)} %get-tuple-element.127, bf16[4,128,256]{2,0,1:T(4,128)(2,1)} %get-tuple-element.126, bf16[4,128,256]{2,0,1:T(4,128)(2,1)} %get-tuple-element.127, bf16[4,128,256]{2,0,1:T(4,128)(2,1)} %get-tuple-element.125, bf16[4,128,256]{2,0,1:T(4,128)(2,1)} %get-tuple-element.126, ...), dimensions={0} | concatenate | bytes 4194304 | tf_op jit(solution)/shard_map/concatenate | solution.py:553
  73.0 5.6 %collective-permute-done.6.refs_20_ = bf16[2048,256]{1,0:T(8,128)(2,1)} collective-permute-done((bf16[2048,256]{1,0:T(8,128)(2,1)}, bf16[2048,256]{1,0:T(8,128)(2,1)}, u32[]{:S(2)}, u32[]{:S(2)}) %collective-permute-start.6) | collective-permute-done | bytes 1048608 | tf_op jit(solution)/shard_map/ppermute | solution.py:439
  79.6 3.5 %collective-permute-start.19 = (bf16[24,64,128]{2,1,0:T(8,128)(2,1)}, bf16[24,64,128]{2,1,0:T(8,128)(2,1)S(1)}, u32[]{:S(2)}, u32[]{:S(2)}) collective-permute-start(bf16[24,64,128]{2,1,0:T(8,128)(2,1)} %copy-done.24), channel_id=1, source_target_pairs={{0,12},{1,13},{2,14},{3,15},{4,8},{5,9},{6,10},{7,11},{8,4},{9,5},... | collective-permute-start | bytes 1179656 | tf_op jit(solution)/shard_map/ppermute | solution.py:439
  87.0 23.6 %fit.3 = (f32[128,64,256]{2,1,0:T(8,128)S(1)}, f32[128,64,256]{2,1,0:T(8,128)S(1)}, bf16[128,64,256]{2,1,0:T(8,128)(2,1)S(1)}, bf16[8192,256]{1,0:T(8,128)(2,1)S(1)}) custom-call(s32[768]{0:T(1024)S(1)} %convert_element_type.49.refs_0_, s32[1536]{0:T(1024)S(1)} %reshape.52.refs_1_, s32[128]{0:T(128)S(1)} %get-tuple-element.74.refs_2_, ...), custom_call_target="tpu_custom_call" | custom-call | flops 2147483648 | bytes 1024 | tf_op jit(solution)/shard_map/fit/pallas_call | solution.py:402
  111.6 3.5 %collective-permute-start.16 = (bf16[24,64,128]{2,1,0:T(8,128)(2,1)S(1)}, bf16[24,64,128]{2,1,0:T(8,128)(2,1)S(1)}, u32[]{:S(2)}, u32[]{:S(2)}) collective-permute-start(bf16[24,64,128]{2,1,0:T(8,128)(2,1)S(1)} %copy-done.19), channel_id=1, source_target_pairs={{0,12},{1,13},{2,14},{3,15},{4,8},{5,9},{6,10},{7,11},{8,4},{9,5},... | collective-permute-start | bytes 1179656 | tf_op jit(solution)/shard_map/ppermute | solution.py:439
  115.1 14.1 %fit.4 = (f32[128,64,256]{2,1,0:T(8,128)S(1)}, f32[128,64,256]{2,1,0:T(8,128)S(1)}) custom-call(s32[768]{0:T(1024)S(1)} %convert_element_type.49.refs_0_, s32[1536]{0:T(1024)S(1)} %reshape.52.refs_1_, s32[128]{0:T(128)S(1)} %get-tuple-element.74.refs_2_, s32[128]{0:T(128)S(1)} %get-tuple-element.75.refs_3_, ...), custom_call_target="tpu_custom_call", output_to_operand_aliasing={{0}: (17, {}), {1}: (18, {})} | custom-call | flops 3221225472 | bytes 1024 | tf_op jit(solution)/shard_map/fit/pallas_call | solution.py:402
  129.2 13.1 %collective-permute-done.15.refs_7_ = bf16[24,64,128]{2,1,0:T(8,128)(2,1)S(1)} collective-permute-done((bf16[24,64,128]{2,1,0:T(8,128)(2,1)S(1)}, bf16[24,64,128]{2,1,0:T(8,128)(2,1)S(1)}, u32[]{:S(2)}, u32[]{:S(2)}) %collective-permute-start.15) | collective-permute-done | bytes 393248 | tf_op jit(solution)/shard_map/ppermute | solution.py:439
  142.4 4.3 %fit.5 = (f32[128,64,256]{2,1,0:T(8,128)S(1)}, f32[128,64,256]{2,1,0:T(8,128)S(1)}, bf16[64,64,256]{2,1,0:T(8,128)(2,1)S(1)}, bf16[32,64,256]{2,1,0:T(8,128)(2,1)S(1)}, bf16[32,64,256]{2,1,0:T(8,128)(2,1)S(1)}) custom-call(s32[768]{0:T(1024)S(1)} %convert_element_type.49.refs_0_, ...), custom_call_target="tpu_custom_call", output_to_operand_aliasing={{0}: (17, {}), {1}: (18, {})} | custom-call | flops 3221225472 | bytes 1024 | tf_op jit(solution)/shard_map/fit/pallas_call | solution.py:402
  148.7 4.2 %collective-permute-done.20 = bf16[64,64,256]{2,1,0:T(8,128)(2,1)S(1)} collective-permute-done((bf16[64,64,256]{2,1,0:T(8,128)(2,1)S(1)}, bf16[64,64,256]{2,1,0:T(8,128)(2,1)S(1)}, u32[]{:S(2)}, u32[]{:S(2)}) %collective-permute-start.20) | collective-permute-done | bytes 2097184 | tf_op jit(solution)/shard_map/ppermute | solution.py:439
  155.2 8.5 %collective-permute-start.24 = (bf16[16,64,256]{2,1,0:T(8,128)(2,1)S(1)}, bf16[16,64,256]{2,1,0:T(8,128)(2,1)S(1)}, u32[]{:S(2)}, u32[]{:S(2)}) collective-permute-start(bf16[16,64,256]{2,1,0:T(8,128)(2,1)S(1)} %get-tuple-element.120), channel_id=1, source_target_pairs={{0,4},{1,5},{2,6},{3,7},{4,0},{5,1},{6,2},{7,3},{8,12},{9,13},{10,... | collective-permute-start | bytes 1572872 | tf_op jit(solution)/shard_map/ppermute | solution.py:439
  163.8 4.2 %collective-permute-done.21 = bf16[16,64,256]{2,1,0:T(8,128)(2,1)S(1)} collective-permute-done((bf16[16,64,256]{2,1,0:T(8,128)(2,1)S(1)}, bf16[16,64,256]{2,1,0:T(8,128)(2,1)S(1)}, u32[]{:S(2)}, u32[]{:S(2)}) %collective-permute-start.21) | collective-permute-done | bytes 524320 | tf_op jit(solution)/shard_map/ppermute | solution.py:439
  168.2 8.0 %collective-permute-done.24 = bf16[16,64,256]{2,1,0:T(8,128)(2,1)S(1)} collective-permute-done((bf16[16,64,256]{2,1,0:T(8,128)(2,1)S(1)}, bf16[16,64,256]{2,1,0:T(8,128)(2,1)S(1)}, u32[]{:S(2)}, u32[]{:S(2)}) %collective-permute-start.24) | collective-permute-done | bytes 524320 | tf_op jit(solution)/shard_map/ppermute | solution.py:439
  176.4 1.8 collective-permute-start.22
  178.2 4.1 %collective-permute-start.25 = (bf16[8,64,256]{2,1,0:T(8,128)(2,1)S(1)}, bf16[8,64,256]{2,1,0:T(8,128)(2,1)S(1)}, u32[]{:S(2)}, u32[]{:S(2)}) collective-permute-start(bf16[8,64,256]{2,1,0:T(8,128)(2,1)S(1)} %slice.131), channel_id=1, source_target_pairs={{0,8},{1,9},{2,10},{3,11},{4,12},{5,13},{6,14},{7,15},{8,0},{9,1},... | collective-permute-start | bytes 786440 | tf_op jit(solution)/shard_map/ppermute | solution.py:439
  183.7 6.4 %collective-permute-done.22 = bf16[8,64,256]{2,1,0:T(8,128)(2,1)S(1)} collective-permute-done((bf16[8,64,256]{2,1,0:T(8,128)(2,1)S(1)}, bf16[8,64,256]{2,1,0:T(8,128)(2,1)S(1)}, u32[]{:S(2)}, u32[]{:S(2)}) %collective-permute-start.22) | collective-permute-done | bytes 262176 | tf_op jit(solution)/shard_map/ppermute | solution.py:439
  190.6 7.2 %collective-permute-start.26 = (bf16[4,64,256]{2,1,0:T(8,128)(2,1)S(1)}, bf16[4,64,256]{2,1,0:T(8,128)(2,1)S(1)}, u32[]{:S(2)}, u32[]{:S(2)}) collective-permute-start(bf16[4,64,256]{2,1,0:T(8,128)(2,1)S(1)} %slice.133), channel_id=1, source_target_pairs={{0,2},{1,3},{2,0},{3,1},{4,6},{5,7},{6,4},{7,5},{8,10},{9,11},{10,... | collective-permute-start | bytes 393224 | tf_op jit(solution)/shard_map/ppermute | solution.py:439
  199.4 10.3 %collective-permute-done.26 = bf16[4,64,256]{2,1,0:T(8,128)(2,1)S(1)} collective-permute-done((bf16[4,64,256]{2,1,0:T(8,128)(2,1)S(1)}, bf16[4,64,256]{2,1,0:T(8,128)(2,1)S(1)}, u32[]{:S(2)}, u32[]{:S(2)}) %collective-permute-start.26) | collective-permute-done | bytes 131104 | tf_op jit(solution)/shard_map/ppermute | solution.py:439
  210.5 1.8 convert_add_fusion.1
  (136 shorter events, 36.9 us)
Async XLA Ops:
  1.7 19.7 %collective-permute-start = (bf16[512,256]{1,0:T(8,128)(2,1)S(1)}, bf16[512,256]{1,0:T(8,128)(2,1)S(1)}, u32[]{:S(2)}, u32[]{:S(2)}) collective-permute-start(bf16[512,256]{1,0:T(8,128)(2,1)S(1)} %bitcast.26), channel_id=1, source_target_pairs={{0,8},{1,9},{2,10},{3,11},{4,12},{5,13},{6,14},{7,15},{8,0},{9,1},... | collective-permute-start | bytes 786440 | tf_op jit(solution)/shard_map/ppermute | solution.py:439
  5.8 53.4 %collective-permute-start.5 = (bf16[32,64,256]{2,1,0:T(8,128)(2,1)}, bf16[32,64,256]{2,1,0:T(8,128)(2,1)S(1)}, u32[]{:S(2)}, u32[]{:S(2)}) collective-permute-start(bf16[32,64,256]{2,1,0:T(8,128)(2,1)} %refs_15_.1), channel_id=1, source_target_pairs={{0,2},{1,3},{2,0},{3,1},{4,6},{5,7},{6,4},{7,5},{8,10},{9,11},{10,... | collective-permute-start | bytes 3145736 | tf_op jit(solution)/shard_map/ppermute | solution.py:439
  21.5 20.6 %collective-permute-start.1 = (bf16[1024,256]{1,0:T(8,128)(2,1)S(1)}, bf16[1024,256]{1,0:T(8,128)(2,1)S(1)}, u32[]{:S(2)}, u32[]{:S(2)}) collective-permute-start(bf16[1024,256]{1,0:T(8,128)(2,1)S(1)} %pad_maximum_fusion.1), channel_id=1, source_target_pairs={{0,4},{1,5},{2,6},{3,7},{4,0},{5,1},{6,2},{7,3},{8,12},{9,13},{10,... | collective-permute-start | bytes 1572872 | tf_op jit(solution)/shard_map/ppermute | solution.py:439
  23.1 31.7 %collective-permute-start.2 = (f32[65,8,128]{2,1,0:T(8,128)S(1)}, f32[65,8,128]{2,1,0:T(8,128)S(1)}, u32[]{:S(2)}, u32[]{:S(2)}) collective-permute-start(f32[65,8,128]{2,1,0:T(8,128)S(1)} %get-tuple-element.64), channel_id=1, source_target_pairs={{0,4},{1,5},{2,6},{3,7},{4,0},{5,1},{6,2},{7,3},{8,12},{9,13},{10,... | collective-permute-start | bytes 798728 | tf_op jit(solution)/shard_map/ppermute | solution.py:439
  23.6 31.2 %collective-permute-start.3 = (f32[65,8,128]{2,1,0:T(8,128)S(1)}, f32[65,8,128]{2,1,0:T(8,128)S(1)}, u32[]{:S(2)}, u32[]{:S(2)}) collective-permute-start(f32[65,8,128]{2,1,0:T(8,128)S(1)} %get-tuple-element.65), channel_id=1, source_target_pairs={{0,8},{1,9},{2,10},{3,11},{4,12},{5,13},{6,14},{7,15},{8,0},{9,1},... | collective-permute-start | bytes 798728 | tf_op jit(solution)/shard_map/ppermute | solution.py:439
  23.9 30.9 %collective-permute-start.4 = (f32[65,8,128]{2,1,0:T(8,128)S(1)}, f32[65,8,128]{2,1,0:T(8,128)S(1)}, u32[]{:S(2)}, u32[]{:S(2)}) collective-permute-start(f32[65,8,128]{2,1,0:T(8,128)S(1)} %get-tuple-element.66), channel_id=1, source_target_pairs={{0,12},{1,13},{2,14},{3,15},{4,8},{5,9},{6,10},{7,11},{8,4},{9,5},... | collective-permute-start | bytes 798728 | tf_op jit(solution)/shard_map/ppermute | solution.py:439
  42.1 36.5 %collective-permute-start.10 = (bf16[32,64,256]{2,1,0:T(8,128)(2,1)}, bf16[32,64,256]{2,1,0:T(8,128)(2,1)}, u32[]{:S(2)}, u32[]{:S(2)}) collective-permute-start(bf16[32,64,256]{2,1,0:T(8,128)(2,1)} %refs_15_.1), channel_id=1, source_target_pairs={{0,1},{1,0},{2,3},{3,2},{4,5},{5,4},{6,7},{7,6},{8,9},{9,8},{10,11... | collective-permute-start | bytes 3145736 | tf_op jit(solution)/shard_map/ppermute | solution.py:439
  54.8 17.7 %collective-permute-start.7 = (bf16[16,64,128]{2,1,0:T(8,128)(2,1)}, bf16[16,64,128]{2,1,0:T(8,128)(2,1)}, u32[]{:S(2)}, u32[]{:S(2)}) collective-permute-start(bf16[16,64,128]{2,1,0:T(8,128)(2,1)} %get-tuple-element.78), channel_id=1, source_target_pairs={{0,4},{1,5},{2,6},{3,7},{4,0},{5,1},{6,2},{7,3},{8,12},{9,13},{10,... | collective-permute-start | bytes 786440 | tf_op jit(solution)/shard_map/ppermute | solution.py:439
  54.8 17.7 %collective-permute-start.8 = (bf16[16,64,128]{2,1,0:T(8,128)(2,1)}, bf16[16,64,128]{2,1,0:T(8,128)(2,1)}, u32[]{:S(2)}, u32[]{:S(2)}) collective-permute-start(bf16[16,64,128]{2,1,0:T(8,128)(2,1)} %get-tuple-element.79), channel_id=1, source_target_pairs={{0,8},{1,9},{2,10},{3,11},{4,12},{5,13},{6,14},{7,15},{8,0},{9,1},... | collective-permute-start | bytes 786440 | tf_op jit(solution)/shard_map/ppermute | solution.py:439
  54.8 18.2 %collective-permute-start.9 = (bf16[16,64,128]{2,1,0:T(8,128)(2,1)}, bf16[16,64,128]{2,1,0:T(8,128)(2,1)}, u32[]{:S(2)}, u32[]{:S(2)}) collective-permute-start(bf16[16,64,128]{2,1,0:T(8,128)(2,1)} %get-tuple-element.80), channel_id=1, source_target_pairs={{0,12},{1,13},{2,14},{3,15},{4,8},{5,9},{6,10},{7,11},{8,4},{9,5},... | collective-permute-start | bytes 786440 | tf_op jit(solution)/shard_map/ppermute | solution.py:439
  59.2 19.4 %collective-permute-start.6 = (bf16[2048,256]{1,0:T(8,128)(2,1)}, bf16[2048,256]{1,0:T(8,128)(2,1)}, u32[]{:S(2)}, u32[]{:S(2)}) collective-permute-start(bf16[2048,256]{1,0:T(8,128)(2,1)} %pad_maximum_fusion.refs_19_), channel_id=1, source_target_pairs={{0,2},{1,3},{2,0},{3,1},{4,6},{5,7},{6,4},{7,5},{8,10},{9,11},{10,... | collective-permute-start | bytes 3145736 | tf_op jit(solution)/shard_map/ppermute | solution.py:439
  78.6 33.0 %collective-permute-start.17 = (bf16[24,64,128]{2,1,0:T(8,128)(2,1)}, bf16[24,64,128]{2,1,0:T(8,128)(2,1)S(1)}, u32[]{:S(2)}, u32[]{:S(2)}) collective-permute-start(bf16[24,64,128]{2,1,0:T(8,128)(2,1)} %copy-done.26), channel_id=1, source_target_pairs={{0,4},{1,5},{2,6},{3,7},{4,0},{5,1},{6,2},{7,3},{8,12},{9,13},{10,... | collective-permute-start | bytes 1179656 | tf_op jit(solution)/shard_map/ppermute | solution.py:439
  78.6 36.5 %collective-permute-start.18 = (bf16[24,64,128]{2,1,0:T(8,128)(2,1)}, bf16[24,64,128]{2,1,0:T(8,128)(2,1)S(1)}, u32[]{:S(2)}, u32[]{:S(2)}) collective-permute-start(bf16[24,64,128]{2,1,0:T(8,128)(2,1)} %copy-done.25), channel_id=1, source_target_pairs={{0,8},{1,9},{2,10},{3,11},{4,12},{5,13},{6,14},{7,15},{8,0},{9,1},... | collective-permute-start | bytes 1179656 | tf_op jit(solution)/shard_map/ppermute | solution.py:439
  79.6 35.5 %collective-permute-start.19 = (bf16[24,64,128]{2,1,0:T(8,128)(2,1)}, bf16[24,64,128]{2,1,0:T(8,128)(2,1)S(1)}, u32[]{:S(2)}, u32[]{:S(2)}) collective-permute-start(bf16[24,64,128]{2,1,0:T(8,128)(2,1)} %copy-done.24), channel_id=1, source_target_pairs={{0,12},{1,13},{2,14},{3,15},{4,8},{5,9},{6,10},{7,11},{8,4},{9,5},... | collective-permute-start | bytes 1179656 | tf_op jit(solution)/shard_map/ppermute | solution.py:439
  110.6 18.6 %collective-permute-start.14 = (bf16[24,64,128]{2,1,0:T(8,128)(2,1)S(1)}, bf16[24,64,128]{2,1,0:T(8,128)(2,1)S(1)}, u32[]{:S(2)}, u32[]{:S(2)}) collective-permute-start(bf16[24,64,128]{2,1,0:T(8,128)(2,1)S(1)} %copy-done.23), channel_id=1, source_target_pairs={{0,4},{1,5},{2,6},{3,7},{4,0},{5,1},{6,2},{7,3},{8,12},{9,13},{10,... | collective-permute-start | bytes 1179656 | tf_op jit(solution)/shard_map/ppermute | solution.py:439
  110.7 31.7 %collective-permute-start.15 = (bf16[24,64,128]{2,1,0:T(8,128)(2,1)S(1)}, bf16[24,64,128]{2,1,0:T(8,128)(2,1)S(1)}, u32[]{:S(2)}, u32[]{:S(2)}) collective-permute-start(bf16[24,64,128]{2,1,0:T(8,128)(2,1)S(1)} %copy-done.21), channel_id=1, source_target_pairs={{0,8},{1,9},{2,10},{3,11},{4,12},{5,13},{6,14},{7,15},{8,0},{9,1},... | collective-permute-start | bytes 1179656 | tf_op jit(solution)/shard_map/ppermute | solution.py:439
  111.6 30.7 %collective-permute-start.16 = (bf16[24,64,128]{2,1,0:T(8,128)(2,1)S(1)}, bf16[24,64,128]{2,1,0:T(8,128)(2,1)S(1)}, u32[]{:S(2)}, u32[]{:S(2)}) collective-permute-start(bf16[24,64,128]{2,1,0:T(8,128)(2,1)S(1)} %copy-done.19), channel_id=1, source_target_pairs={{0,12},{1,13},{2,14},{3,15},{4,8},{5,9},{6,10},{7,11},{8,4},{9,5},... | collective-permute-start | bytes 1179656 | tf_op jit(solution)/shard_map/ppermute | solution.py:439
  154.0 14.0 %collective-permute-start.21 = (bf16[16,64,256]{2,1,0:T(8,128)(2,1)S(1)}, bf16[16,64,256]{2,1,0:T(8,128)(2,1)S(1)}, u32[]{:S(2)}, u32[]{:S(2)}) collective-permute-start(bf16[16,64,256]{2,1,0:T(8,128)(2,1)S(1)} %get-tuple-element.121), channel_id=1, source_target_pairs={{0,2},{1,3},{2,0},{3,1},{4,6},{5,7},{6,4},{7,5},{8,10},{9,11},{10,... | collective-permute-start | bytes 1572872 | tf_op jit(solution)/shard_map/ppermute | solution.py:439
  155.1 27.2 %collective-permute-start.28 = (bf16[32,64,256]{2,1,0:T(8,128)(2,1)S(1)}, bf16[32,64,256]{2,1,0:T(8,128)(2,1)S(1)}, u32[]{:S(2)}, u32[]{:S(2)}) collective-permute-start(bf16[32,64,256]{2,1,0:T(8,128)(2,1)S(1)} %copy-done.17), channel_id=1, source_target_pairs={{0,1},{1,0},{2,3},{3,2},{4,5},{5,4},{6,7},{7,6},{8,9},{9,8},{10,11... | collective-permute-start | bytes 3145736 | tf_op jit(solution)/shard_map/ppermute | solution.py:439
  155.2 21.0 %collective-permute-start.24 = (bf16[16,64,256]{2,1,0:T(8,128)(2,1)S(1)}, bf16[16,64,256]{2,1,0:T(8,128)(2,1)S(1)}, u32[]{:S(2)}, u32[]{:S(2)}) collective-permute-start(bf16[16,64,256]{2,1,0:T(8,128)(2,1)S(1)} %get-tuple-element.120), channel_id=1, source_target_pairs={{0,4},{1,5},{2,6},{3,7},{4,0},{5,1},{6,2},{7,3},{8,12},{9,13},{10,... | collective-permute-start | bytes 1572872 | tf_op jit(solution)/shard_map/ppermute | solution.py:439
  163.8 46.8 %collective-permute-start.27 = (bf16[32,64,256]{2,1,0:T(8,128)(2,1)S(1)}, bf16[32,64,256]{2,1,0:T(8,128)(2,1)S(1)}, u32[]{:S(2)}, u32[]{:S(2)}) collective-permute-start(bf16[32,64,256]{2,1,0:T(8,128)(2,1)S(1)} %copy-done.15), channel_id=1, source_target_pairs={{0,1},{1,0},{2,3},{3,2},{4,5},{5,4},{6,7},{7,6},{8,9},{9,8},{10,11... | collective-permute-start | bytes 3145736 | tf_op jit(solution)/shard_map/ppermute | solution.py:439
  176.4 13.7 %collective-permute-start.22 = (bf16[8,64,256]{2,1,0:T(8,128)(2,1)S(1)}, bf16[8,64,256]{2,1,0:T(8,128)(2,1)S(1)}, u32[]{:S(2)}, u32[]{:S(2)}) collective-permute-start(bf16[8,64,256]{2,1,0:T(8,128)(2,1)S(1)} %slice.132), channel_id=1, source_target_pairs={{0,4},{1,5},{2,6},{3,7},{4,0},{5,1},{6,2},{7,3},{8,12},{9,13},{10,... | collective-permute-start | bytes 786440 | tf_op jit(solution)/shard_map/ppermute | solution.py:439
  182.7 27.9 %collective-permute-start.29 = (bf16[32,64,256]{2,1,0:T(8,128)(2,1)S(1)}, bf16[32,64,256]{2,1,0:T(8,128)(2,1)S(1)}, u32[]{:S(2)}, u32[]{:S(2)}) collective-permute-start(bf16[32,64,256]{2,1,0:T(8,128)(2,1)S(1)} %add_convert_fusion), channel_id=1, source_target_pairs={{0,2},{1,3},{2,0},{3,1},{4,6},{5,7},{6,4},{7,5},{8,10},{9,11},{10,... | collective-permute-start | bytes 3145736 | tf_op jit(solution)/shard_map/ppermute | solution.py:439
  190.6 19.0 %collective-permute-start.26 = (bf16[4,64,256]{2,1,0:T(8,128)(2,1)S(1)}, bf16[4,64,256]{2,1,0:T(8,128)(2,1)S(1)}, u32[]{:S(2)}, u32[]{:S(2)}) collective-permute-start(bf16[4,64,256]{2,1,0:T(8,128)(2,1)S(1)} %slice.133), channel_id=1, source_target_pairs={{0,2},{1,3},{2,0},{3,1},{4,6},{5,7},{6,4},{7,5},{8,10},{9,11},{10,... | collective-permute-start | bytes 393224 | tf_op jit(solution)/shard_map/ppermute | solution.py:439
  (36 other events, 297.6 us)

commit v2 on v1

--- a/solution.py
+++ b/solution.py
@@ -511,8 +511,6 @@
     sizes = round_sizes(slots)
 
     held = jnp.swapaxes(stress.reshape(epochs, local, PBLK), 0, 1).reshape(-1, PBLK)
-    other = partner(held, devices, devices // 2)
-    across_screens = partner(screens, devices, PAIR)
     obs, pix = pack(
         observations,
         pixel_geometry,
@@ -523,18 +521,19 @@
         local_tiles,
     )
 
+    _, held = lax.optimization_barrier((pix, held))
+    other = partner(held, devices, devices // 2)
+    across_screens = partner(screens, devices, PAIR)
     def exchange(parts):
         got = [partner(parts[x], devices, x * LAYER) for x in range(layers - 1, 0, -1)]
         return [parts[0]] + got[::-1]
 
+    pix = exchange(pix)
     distance = devices // 2
     while distance >= LAYER:
         if distance < devices // 2:
             other = partner(held, devices, distance)
         held = jnp.concatenate([held, other], axis=0)
-        if distance == devices // 2:
-            _, pix = lax.optimization_barrier((held, pix))
-            pix = exchange(pix)
         distance //= 2
     patch_blocks = devices * local
     east, north, depth, compliance = patch_geometry

time: 213 us -> 224 us (1.052)
  waiting for transfers between devices: 78.5 us -> 93.4 us
  starting transfers between devices: 49.6 us -> 43.9 us
    ppermute x30, waiting for transfers between devices: 78.5 us -> 93.4 us  [partner(): lax.ppermute(values, 'tile', [(i, i ^ distance) for i in range(devices)])]
    ppermute x30, starting transfers between devices: 49.6 us -> 43.9 us  [partner(): lax.ppermute(values, 'tile', [(i, i ^ distance) for i in range(devices)])]
  transfers between devices with their start and end apart: 30 -> 30, of which waited for: 10 -> 12; matrix products, arithmetic and copies ran while one was open for 9% -> 8% of each run, Pallas kernels for 20% -> 17%
where the time goes in v2:
time: 224 us; the launch traced here: 223 us
  waiting for transfers between devices  93.4 us (42%)
  Pallas kernels  47 us (21%)
  starting transfers between devices  43.9 us (20%)
  local copies, waits for them, and re-layouts  29.3 us (13%)
  other arithmetic  8.62 us (4%)
    ppermute x30, waiting for transfers between devices, partner(): lax.ppermute(values, 'tile', [(i, i ^ distance) for i in range(devices)])  93.4 us
    ppermute x30, starting transfers between devices, partner(): lax.ppermute(values, 'tile', [(i, i ^ distance) for i in range(devices)])  43.9 us
    pallas_call x3, Pallas kernels, fit(): pl.pallas_call(functools.partial(fit_kernel, first, final, layers, slots,...  42.1 us
    unnamed x59, local copies, waits for them, and re-layouts  16 us
    concatenate x1, local copies, waits for them, and re-layouts, on_device(): jnp.concatenate([faces[second] for _, second in CROSS] + [jnp.zeros((8,)...  8.03 us
    pallas_call x1, Pallas kernels, pack(): pl.pallas_call(functools.partial(pack_kernel, local_tiles, layers, slots)...  4.98 us
  transfers between devices with their start and end apart: 30, of which 12 were waited for; matrix products, arithmetic and copies ran while one was open for 8% of the time, Pallas kernels for 17%

profile of v2, /device:TPU:0, one launch (start us, length us, event | category | flops | bytes accessed | tf_op | source)
XLA Modules:
  0.0 223.2 jit_solution(16715856916055384298)
XLA Ops:
  5.6 5.0 %pack.1 = (bf16[16,64,128]{2,1,0:T(8,128)(2,1)S(1)}, bf16[16,64,128]{2,1,0:T(8,128)(2,1)}, bf16[16,64,128]{2,1,0:T(8,128)(2,1)}, bf16[16,64,128]{2,1,0:T(8,128)(...) custom-call(s32[1]{0:T(128)} %bitcast.here, ...), custom_call_target="tpu_custom_call" | custom-call | tf_op jit(solution)/shard_map/pack/pallas_call | solution.py:96
  17.4 4.0 %collective-permute-start = (bf16[512,256]{1,0:T(8,128)(2,1)S(1)}, bf16[512,256]{1,0:T(8,128)(2,1)S(1)}, u32[]{:S(2)}, u32[]{:S(2)}) collective-permute-start(bf16[512,256]{1,0:T(8,128)(2,1)S(1)} %bitcast.26), channel_id=1, source_target_pairs={{0,8},{1,9},{2,10},{3,11},{4,12},{5,13},{6,14},{7,15},{8,0},{9,1},... | collective-permute-start | bytes 786440 | tf_op jit(solution)/shard_map/ppermute | solution.py:439
  23.3 2.5 %collective-permute-start.4 = (f32[65,8,128]{2,1,0:T(8,128)S(1)}, f32[65,8,128]{2,1,0:T(8,128)S(1)}, u32[]{:S(2)}, u32[]{:S(2)}) collective-permute-start(f32[65,8,128]{2,1,0:T(8,128)S(1)} %get-tuple-element.59), channel_id=1, source_target_pairs={{0,12},{1,13},{2,14},{3,15},{4,8},{5,9},{6,10},{7,11},{8,4},{9,5},... | collective-permute-start | bytes 798728 | tf_op jit(solution)/shard_map/ppermute | solution.py:439
  27.9 7.1 %collective-permute-done = bf16[512,256]{1,0:T(8,128)(2,1)S(1)} collective-permute-done((bf16[512,256]{1,0:T(8,128)(2,1)S(1)}, bf16[512,256]{1,0:T(8,128)(2,1)S(1)}, u32[]{:S(2)}, u32[]{:S(2)}) %collective-permute-start) | collective-permute-done | bytes 262176 | tf_op jit(solution)/shard_map/ppermute | solution.py:439
  36.1 21.0 %collective-permute-done.1 = bf16[1024,256]{1,0:T(8,128)(2,1)S(1)} collective-permute-done((bf16[1024,256]{1,0:T(8,128)(2,1)S(1)}, bf16[1024,256]{1,0:T(8,128)(2,1)S(1)}, u32[]{:S(2)}, u32[]{:S(2)}) %collective-permute-start.1) | collective-permute-done | bytes 524320 | tf_op jit(solution)/shard_map/ppermute | solution.py:439
  59.0 5.5 %collective-permute-start.8 = (bf16[16,64,128]{2,1,0:T(8,128)(2,1)}, bf16[16,64,128]{2,1,0:T(8,128)(2,1)}, u32[]{:S(2)}, u32[]{:S(2)}) collective-permute-start(bf16[16,64,128]{2,1,0:T(8,128)(2,1)} %get-tuple-element.73), channel_id=1, source_target_pairs={{0,8},{1,9},{2,10},{3,11},{4,12},{5,13},{6,14},{7,15},{8,0},{9,1},... | collective-permute-start | bytes 786440 | tf_op jit(solution)/shard_map/ppermute | solution.py:439
  70.3 8.0 %concatenate.21 = bf16[32,128,256]{2,0,1:T(8,128)(2,1)S(1)} concatenate(bf16[4,128,256]{2,0,1:T(4,128)(2,1)} %get-tuple-element.121, bf16[4,128,256]{2,0,1:T(4,128)(2,1)} %get-tuple-element.120, bf16[4,128,256]{2,0,1:T(4,128)(2,1)} %get-tuple-element.121, bf16[4,128,256]{2,0,1:T(4,128)(2,1)} %get-tuple-element.119, bf16[4,128,256]{2,0,1:T(4,128)(2,1)} %get-tuple-element.120, ...), dimensions={0} | concatenate | bytes 4194304 | tf_op jit(solution)/shard_map/concatenate | solution.py:552
  79.1 4.1 %collective-permute-done.8.refs_7_ = bf16[16,64,128]{2,1,0:T(8,128)(2,1)} collective-permute-done((bf16[16,64,128]{2,1,0:T(8,128)(2,1)}, bf16[16,64,128]{2,1,0:T(8,128)(2,1)}, u32[]{:S(2)}, u32[]{:S(2)}) %collective-permute-start.8) | collective-permute-done | bytes 262176 | tf_op jit(solution)/shard_map/ppermute | solution.py:439
  83.2 6.7 %collective-permute-done.6.refs_20_ = bf16[2048,256]{1,0:T(8,128)(2,1)} collective-permute-done((bf16[2048,256]{1,0:T(8,128)(2,1)}, bf16[2048,256]{1,0:T(8,128)(2,1)}, u32[]{:S(2)}, u32[]{:S(2)}) %collective-permute-start.6) | collective-permute-done | bytes 1048608 | tf_op jit(solution)/shard_map/ppermute | solution.py:439
  90.5 3.5 %collective-permute-start.18 = (bf16[24,64,128]{2,1,0:T(8,128)(2,1)}, bf16[24,64,128]{2,1,0:T(8,128)(2,1)S(1)}, u32[]{:S(2)}, u32[]{:S(2)}) collective-permute-start(bf16[24,64,128]{2,1,0:T(8,128)(2,1)} %copy-done.25), channel_id=1, source_target_pairs={{0,8},{1,9},{2,10},{3,11},{4,12},{5,13},{6,14},{7,15},{8,0},{9,1},... | collective-permute-start | bytes 1179656 | tf_op jit(solution)/shard_map/ppermute | solution.py:439
  98.3 23.6 %fit.3 = (f32[128,64,256]{2,1,0:T(8,128)S(1)}, f32[128,64,256]{2,1,0:T(8,128)S(1)}, bf16[128,64,256]{2,1,0:T(8,128)(2,1)S(1)}, bf16[8192,256]{1,0:T(8,128)(2,1)S(1)}) custom-call(s32[768]{0:T(1024)S(1)} %convert_element_type.49.refs_0_, s32[1536]{0:T(1024)S(1)} %reshape.52.refs_1_, s32[128]{0:T(128)S(1)} %get-tuple-element.68.refs_2_, ...), custom_call_target="tpu_custom_call" | custom-call | flops 2147483648 | bytes 1024 | tf_op jit(solution)/shard_map/fit/pallas_call | solution.py:402
  122.3 3.7 %collective-permute-start.15 = (bf16[24,64,128]{2,1,0:T(8,128)(2,1)S(1)}, bf16[24,64,128]{2,1,0:T(8,128)(2,1)S(1)}, u32[]{:S(2)}, u32[]{:S(2)}) collective-permute-start(bf16[24,64,128]{2,1,0:T(8,128)(2,1)S(1)} %copy-done.21), channel_id=1, source_target_pairs={{0,8},{1,9},{2,10},{3,11},{4,12},{5,13},{6,14},{7,15},{8,0},{9,1},... | collective-permute-start | bytes 1179656 | tf_op jit(solution)/shard_map/ppermute | solution.py:439
  126.5 14.2 %fit.4 = (f32[128,64,256]{2,1,0:T(8,128)S(1)}, f32[128,64,256]{2,1,0:T(8,128)S(1)}) custom-call(s32[768]{0:T(1024)S(1)} %convert_element_type.49.refs_0_, s32[1536]{0:T(1024)S(1)} %reshape.52.refs_1_, s32[128]{0:T(128)S(1)} %get-tuple-element.68.refs_2_, s32[128]{0:T(128)S(1)} %get-tuple-element.69.refs_3_, ...), custom_call_target="tpu_custom_call", output_to_operand_aliasing={{0}: (17, {}), {1}: (18, {})} | custom-call | flops 3221225472 | bytes 1024 | tf_op jit(solution)/shard_map/fit/pallas_call | solution.py:402
  140.6 14.1 %collective-permute-done.15.refs_7_ = bf16[24,64,128]{2,1,0:T(8,128)(2,1)S(1)} collective-permute-done((bf16[24,64,128]{2,1,0:T(8,128)(2,1)S(1)}, bf16[24,64,128]{2,1,0:T(8,128)(2,1)S(1)}, u32[]{:S(2)}, u32[]{:S(2)}) %collective-permute-start.15) | collective-permute-done | bytes 393248 | tf_op jit(solution)/shard_map/ppermute | solution.py:439
  154.8 4.3 %fit.5 = (f32[128,64,256]{2,1,0:T(8,128)S(1)}, f32[128,64,256]{2,1,0:T(8,128)S(1)}, bf16[64,64,256]{2,1,0:T(8,128)(2,1)S(1)}, bf16[32,64,256]{2,1,0:T(8,128)(2,1)S(1)}, bf16[32,64,256]{2,1,0:T(8,128)(2,1)S(1)}) custom-call(s32[768]{0:T(1024)S(1)} %convert_element_type.49.refs_0_, ...), custom_call_target="tpu_custom_call", output_to_operand_aliasing={{0}: (17, {}), {1}: (18, {})} | custom-call | flops 3221225472 | bytes 1024 | tf_op jit(solution)/shard_map/fit/pallas_call | solution.py:402
  161.0 4.2 %collective-permute-done.20 = bf16[64,64,256]{2,1,0:T(8,128)(2,1)S(1)} collective-permute-done((bf16[64,64,256]{2,1,0:T(8,128)(2,1)S(1)}, bf16[64,64,256]{2,1,0:T(8,128)(2,1)S(1)}, u32[]{:S(2)}, u32[]{:S(2)}) %collective-permute-start.20) | collective-permute-done | bytes 2097184 | tf_op jit(solution)/shard_map/ppermute | solution.py:439
  168.0 10.5 %collective-permute-start.24 = (bf16[16,64,256]{2,1,0:T(8,128)(2,1)S(1)}, bf16[16,64,256]{2,1,0:T(8,128)(2,1)S(1)}, u32[]{:S(2)}, u32[]{:S(2)}) collective-permute-start(bf16[16,64,256]{2,1,0:T(8,128)(2,1)S(1)} %get-tuple-element.114), channel_id=1, source_target_pairs={{0,4},{1,5},{2,6},{3,7},{4,0},{5,1},{6,2},{7,3},{8,12},{9,13},{10,... | collective-permute-start | bytes 1572872 | tf_op jit(solution)/shard_map/ppermute | solution.py:439
  178.5 1.9 collective-permute-done.21
  180.6 10.3 %collective-permute-done.24 = bf16[16,64,256]{2,1,0:T(8,128)(2,1)S(1)} collective-permute-done((bf16[16,64,256]{2,1,0:T(8,128)(2,1)S(1)}, bf16[16,64,256]{2,1,0:T(8,128)(2,1)S(1)}, u32[]{:S(2)}, u32[]{:S(2)}) %collective-permute-start.24) | collective-permute-done | bytes 524320 | tf_op jit(solution)/shard_map/ppermute | solution.py:439
  191.1 1.8 collective-permute-start.22
  194.4 8.7 %collective-permute-done.22 = bf16[8,64,256]{2,1,0:T(8,128)(2,1)S(1)} collective-permute-done((bf16[8,64,256]{2,1,0:T(8,128)(2,1)S(1)}, bf16[8,64,256]{2,1,0:T(8,128)(2,1)S(1)}, u32[]{:S(2)}, u32[]{:S(2)}) %collective-permute-start.22) | collective-permute-done | bytes 262176 | tf_op jit(solution)/shard_map/ppermute | solution.py:439
  203.8 7.3 %collective-permute-done.25 = bf16[8,64,256]{2,1,0:T(8,128)(2,1)S(1)} collective-permute-done((bf16[8,64,256]{2,1,0:T(8,128)(2,1)S(1)}, bf16[8,64,256]{2,1,0:T(8,128)(2,1)S(1)}, u32[]{:S(2)}, u32[]{:S(2)}) %collective-permute-start.25) | collective-permute-done | bytes 262176 | tf_op jit(solution)/shard_map/ppermute | solution.py:439
  212.6 7.9 %collective-permute-done.26 = bf16[4,64,256]{2,1,0:T(8,128)(2,1)S(1)} collective-permute-done((bf16[4,64,256]{2,1,0:T(8,128)(2,1)S(1)}, bf16[4,64,256]{2,1,0:T(8,128)(2,1)S(1)}, u32[]{:S(2)}, u32[]{:S(2)}) %collective-permute-start.26) | collective-permute-done | bytes 131104 | tf_op jit(solution)/shard_map/ppermute | solution.py:439
  221.4 1.8 convert_add_fusion.1
  (136 shorter events, 40.6 us)
Async XLA Ops:
  17.4 17.6 %collective-permute-start = (bf16[512,256]{1,0:T(8,128)(2,1)S(1)}, bf16[512,256]{1,0:T(8,128)(2,1)S(1)}, u32[]{:S(2)}, u32[]{:S(2)}) collective-permute-start(bf16[512,256]{1,0:T(8,128)(2,1)S(1)} %bitcast.26), channel_id=1, source_target_pairs={{0,8},{1,9},{2,10},{3,11},{4,12},{5,13},{6,14},{7,15},{8,0},{9,1},... | collective-permute-start | bytes 786440 | tf_op jit(solution)/shard_map/ppermute | solution.py:439
  21.4 36.7 %collective-permute-start.2 = (f32[65,8,128]{2,1,0:T(8,128)S(1)}, f32[65,8,128]{2,1,0:T(8,128)S(1)}, u32[]{:S(2)}, u32[]{:S(2)}) collective-permute-start(f32[65,8,128]{2,1,0:T(8,128)S(1)} %get-tuple-element.57), channel_id=1, source_target_pairs={{0,4},{1,5},{2,6},{3,7},{4,0},{5,1},{6,2},{7,3},{8,12},{9,13},{10,... | collective-permute-start | bytes 798728 | tf_op jit(solution)/shard_map/ppermute | solution.py:439
  23.0 36.0 %collective-permute-start.3 = (f32[65,8,128]{2,1,0:T(8,128)S(1)}, f32[65,8,128]{2,1,0:T(8,128)S(1)}, u32[]{:S(2)}, u32[]{:S(2)}) collective-permute-start(f32[65,8,128]{2,1,0:T(8,128)S(1)} %get-tuple-element.58), channel_id=1, source_target_pairs={{0,8},{1,9},{2,10},{3,11},{4,12},{5,13},{6,14},{7,15},{8,0},{9,1},... | collective-permute-start | bytes 798728 | tf_op jit(solution)/shard_map/ppermute | solution.py:439
  23.3 41.2 %collective-permute-start.4 = (f32[65,8,128]{2,1,0:T(8,128)S(1)}, f32[65,8,128]{2,1,0:T(8,128)S(1)}, u32[]{:S(2)}, u32[]{:S(2)}) collective-permute-start(f32[65,8,128]{2,1,0:T(8,128)S(1)} %get-tuple-element.59), channel_id=1, source_target_pairs={{0,12},{1,13},{2,14},{3,15},{4,8},{5,9},{6,10},{7,11},{8,4},{9,5},... | collective-permute-start | bytes 798728 | tf_op jit(solution)/shard_map/ppermute | solution.py:439
  25.8 38.8 %collective-permute-start.5 = (bf16[32,64,256]{2,1,0:T(8,128)(2,1)}, bf16[32,64,256]{2,1,0:T(8,128)(2,1)S(1)}, u32[]{:S(2)}, u32[]{:S(2)}) collective-permute-start(bf16[32,64,256]{2,1,0:T(8,128)(2,1)} %refs_15_.1), channel_id=1, source_target_pairs={{0,2},{1,3},{2,0},{3,1},{4,6},{5,7},{6,4},{7,5},{8,10},{9,11},{10,... | collective-permute-start | bytes 3145736 | tf_op jit(solution)/shard_map/ppermute | solution.py:439
  35.0 22.0 %collective-permute-start.1 = (bf16[1024,256]{1,0:T(8,128)(2,1)S(1)}, bf16[1024,256]{1,0:T(8,128)(2,1)S(1)}, u32[]{:S(2)}, u32[]{:S(2)}) collective-permute-start(bf16[1024,256]{1,0:T(8,128)(2,1)S(1)} %pad_maximum_fusion.1), channel_id=1, source_target_pairs={{0,4},{1,5},{2,6},{3,7},{4,0},{5,1},{6,2},{7,3},{8,12},{9,13},{10,... | collective-permute-start | bytes 1572872 | tf_op jit(solution)/shard_map/ppermute | solution.py:439
  57.0 33.5 %collective-permute-start.10 = (bf16[32,64,256]{2,1,0:T(8,128)(2,1)}, bf16[32,64,256]{2,1,0:T(8,128)(2,1)}, u32[]{:S(2)}, u32[]{:S(2)}) collective-permute-start(bf16[32,64,256]{2,1,0:T(8,128)(2,1)} %refs_15_.1), channel_id=1, source_target_pairs={{0,1},{1,0},{2,3},{3,2},{4,5},{5,4},{6,7},{7,6},{8,9},{9,8},{10,11... | collective-permute-start | bytes 3145736 | tf_op jit(solution)/shard_map/ppermute | solution.py:439
  58.1 21.0 %collective-permute-start.7 = (bf16[16,64,128]{2,1,0:T(8,128)(2,1)}, bf16[16,64,128]{2,1,0:T(8,128)(2,1)}, u32[]{:S(2)}, u32[]{:S(2)}) collective-permute-start(bf16[16,64,128]{2,1,0:T(8,128)(2,1)} %get-tuple-element.72), channel_id=1, source_target_pairs={{0,4},{1,5},{2,6},{3,7},{4,0},{5,1},{6,2},{7,3},{8,12},{9,13},{10,... | collective-permute-start | bytes 786440 | tf_op jit(solution)/shard_map/ppermute | solution.py:439
  59.0 24.2 %collective-permute-start.8 = (bf16[16,64,128]{2,1,0:T(8,128)(2,1)}, bf16[16,64,128]{2,1,0:T(8,128)(2,1)}, u32[]{:S(2)}, u32[]{:S(2)}) collective-permute-start(bf16[16,64,128]{2,1,0:T(8,128)(2,1)} %get-tuple-element.73), channel_id=1, source_target_pairs={{0,8},{1,9},{2,10},{3,11},{4,12},{5,13},{6,14},{7,15},{8,0},{9,1},... | collective-permute-start | bytes 786440 | tf_op jit(solution)/shard_map/ppermute | solution.py:439
  64.6 18.7 %collective-permute-start.9 = (bf16[16,64,128]{2,1,0:T(8,128)(2,1)}, bf16[16,64,128]{2,1,0:T(8,128)(2,1)}, u32[]{:S(2)}, u32[]{:S(2)}) collective-permute-start(bf16[16,64,128]{2,1,0:T(8,128)(2,1)} %get-tuple-element.74), channel_id=1, source_target_pairs={{0,12},{1,13},{2,14},{3,15},{4,8},{5,9},{6,10},{7,11},{8,4},{9,5},... | collective-permute-start | bytes 786440 | tf_op jit(solution)/shard_map/ppermute | solution.py:439
  64.6 25.4 %collective-permute-start.6 = (bf16[2048,256]{1,0:T(8,128)(2,1)}, bf16[2048,256]{1,0:T(8,128)(2,1)}, u32[]{:S(2)}, u32[]{:S(2)}) collective-permute-start(bf16[2048,256]{1,0:T(8,128)(2,1)} %pad_maximum_fusion.refs_19_), channel_id=1, source_target_pairs={{0,2},{1,3},{2,0},{3,1},{4,6},{5,7},{6,4},{7,5},{8,10},{9,11},{10,... | collective-permute-start | bytes 3145736 | tf_op jit(solution)/shard_map/ppermute | solution.py:439
  79.1 14.9 %collective-permute-start.11 = (bf16[32,64,256]{2,1,0:T(8,128)(2,1)}, bf16[32,64,256]{2,1,0:T(8,128)(2,1)S(1)}, u32[]{:S(2)}, u32[]{:S(2)}) collective-permute-start(bf16[32,64,256]{2,1,0:T(8,128)(2,1)} %copy-done.3), channel_id=1, source_target_pairs={{0,1},{1,0},{2,3},{3,2},{4,5},{5,4},{6,7},{7,6},{8,9},{9,8},{10,11... | collective-permute-start | bytes 3145736 | tf_op jit(solution)/shard_map/ppermute | solution.py:439
  90.0 36.1 %collective-permute-start.17 = (bf16[24,64,128]{2,1,0:T(8,128)(2,1)}, bf16[24,64,128]{2,1,0:T(8,128)(2,1)S(1)}, u32[]{:S(2)}, u32[]{:S(2)}) collective-permute-start(bf16[24,64,128]{2,1,0:T(8,128)(2,1)} %copy-done.26), channel_id=1, source_target_pairs={{0,4},{1,5},{2,6},{3,7},{4,0},{5,1},{6,2},{7,3},{8,12},{9,13},{10,... | collective-permute-start | bytes 1179656 | tf_op jit(solution)/shard_map/ppermute | solution.py:439
  90.5 35.9 %collective-permute-start.18 = (bf16[24,64,128]{2,1,0:T(8,128)(2,1)}, bf16[24,64,128]{2,1,0:T(8,128)(2,1)S(1)}, u32[]{:S(2)}, u32[]{:S(2)}) collective-permute-start(bf16[24,64,128]{2,1,0:T(8,128)(2,1)} %copy-done.25), channel_id=1, source_target_pairs={{0,8},{1,9},{2,10},{3,11},{4,12},{5,13},{6,14},{7,15},{8,0},{9,1},... | collective-permute-start | bytes 1179656 | tf_op jit(solution)/shard_map/ppermute | solution.py:439
  94.0 32.4 %collective-permute-start.19 = (bf16[24,64,128]{2,1,0:T(8,128)(2,1)}, bf16[24,64,128]{2,1,0:T(8,128)(2,1)S(1)}, u32[]{:S(2)}, u32[]{:S(2)}) collective-permute-start(bf16[24,64,128]{2,1,0:T(8,128)(2,1)} %copy-done.24), channel_id=1, source_target_pairs={{0,12},{1,13},{2,14},{3,15},{4,8},{5,9},{6,10},{7,11},{8,4},{9,5},... | collective-permute-start | bytes 1179656 | tf_op jit(solution)/shard_map/ppermute | solution.py:439
  122.0 18.6 %collective-permute-start.14 = (bf16[24,64,128]{2,1,0:T(8,128)(2,1)S(1)}, bf16[24,64,128]{2,1,0:T(8,128)(2,1)S(1)}, u32[]{:S(2)}, u32[]{:S(2)}) collective-permute-start(bf16[24,64,128]{2,1,0:T(8,128)(2,1)S(1)} %copy-done.23), channel_id=1, source_target_pairs={{0,4},{1,5},{2,6},{3,7},{4,0},{5,1},{6,2},{7,3},{8,12},{9,13},{10,... | collective-permute-start | bytes 1179656 | tf_op jit(solution)/shard_map/ppermute | solution.py:439
  122.3 32.5 %collective-permute-start.15 = (bf16[24,64,128]{2,1,0:T(8,128)(2,1)S(1)}, bf16[24,64,128]{2,1,0:T(8,128)(2,1)S(1)}, u32[]{:S(2)}, u32[]{:S(2)}) collective-permute-start(bf16[24,64,128]{2,1,0:T(8,128)(2,1)S(1)} %copy-done.21), channel_id=1, source_target_pairs={{0,8},{1,9},{2,10},{3,11},{4,12},{5,13},{6,14},{7,15},{8,0},{9,1},... | collective-permute-start | bytes 1179656 | tf_op jit(solution)/shard_map/ppermute | solution.py:439
  126.0 28.7 %collective-permute-start.16 = (bf16[24,64,128]{2,1,0:T(8,128)(2,1)S(1)}, bf16[24,64,128]{2,1,0:T(8,128)(2,1)S(1)}, u32[]{:S(2)}, u32[]{:S(2)}) collective-permute-start(bf16[24,64,128]{2,1,0:T(8,128)(2,1)S(1)} %copy-done.19), channel_id=1, source_target_pairs={{0,12},{1,13},{2,14},{3,15},{4,8},{5,9},{6,10},{7,11},{8,4},{9,5},... | collective-permute-start | bytes 1179656 | tf_op jit(solution)/shard_map/ppermute | solution.py:439
  166.4 14.0 %collective-permute-start.21 = (bf16[16,64,256]{2,1,0:T(8,128)(2,1)S(1)}, bf16[16,64,256]{2,1,0:T(8,128)(2,1)S(1)}, u32[]{:S(2)}, u32[]{:S(2)}) collective-permute-start(bf16[16,64,256]{2,1,0:T(8,128)(2,1)S(1)} %get-tuple-element.115), channel_id=1, source_target_pairs={{0,2},{1,3},{2,0},{3,1},{4,6},{5,7},{6,4},{7,5},{8,10},{9,11},{10,... | collective-permute-start | bytes 1572872 | tf_op jit(solution)/shard_map/ppermute | solution.py:439
  168.0 25.0 %collective-permute-start.28 = (bf16[32,64,256]{2,1,0:T(8,128)(2,1)S(1)}, bf16[32,64,256]{2,1,0:T(8,128)(2,1)S(1)}, u32[]{:S(2)}, u32[]{:S(2)}) collective-permute-start(bf16[32,64,256]{2,1,0:T(8,128)(2,1)S(1)} %copy-done.17), channel_id=1, source_target_pairs={{0,1},{1,0},{2,3},{3,2},{4,5},{5,4},{6,7},{7,6},{8,9},{9,8},{10,11... | collective-permute-start | bytes 3145736 | tf_op jit(solution)/shard_map/ppermute | solution.py:439
  168.0 22.9 %collective-permute-start.24 = (bf16[16,64,256]{2,1,0:T(8,128)(2,1)S(1)}, bf16[16,64,256]{2,1,0:T(8,128)(2,1)S(1)}, u32[]{:S(2)}, u32[]{:S(2)}) collective-permute-start(bf16[16,64,256]{2,1,0:T(8,128)(2,1)S(1)} %get-tuple-element.114), channel_id=1, source_target_pairs={{0,4},{1,5},{2,6},{3,7},{4,0},{5,1},{6,2},{7,3},{8,12},{9,13},{10,... | collective-permute-start | bytes 1572872 | tf_op jit(solution)/shard_map/ppermute | solution.py:439
  178.5 43.0 %collective-permute-start.27 = (bf16[32,64,256]{2,1,0:T(8,128)(2,1)S(1)}, bf16[32,64,256]{2,1,0:T(8,128)(2,1)S(1)}, u32[]{:S(2)}, u32[]{:S(2)}) collective-permute-start(bf16[32,64,256]{2,1,0:T(8,128)(2,1)S(1)} %copy-done.15), channel_id=1, source_target_pairs={{0,1},{1,0},{2,3},{3,2},{4,5},{5,4},{6,7},{7,6},{8,9},{9,8},{10,11... | collective-permute-start | bytes 3145736 | tf_op jit(solution)/shard_map/ppermute | solution.py:439
  192.9 18.2 %collective-permute-start.25 = (bf16[8,64,256]{2,1,0:T(8,128)(2,1)S(1)}, bf16[8,64,256]{2,1,0:T(8,128)(2,1)S(1)}, u32[]{:S(2)}, u32[]{:S(2)}) collective-permute-start(bf16[8,64,256]{2,1,0:T(8,128)(2,1)S(1)} %slice.131), channel_id=1, source_target_pairs={{0,8},{1,9},{2,10},{3,11},{4,12},{5,13},{6,14},{7,15},{8,0},{9,1},... | collective-permute-start | bytes 786440 | tf_op jit(solution)/shard_map/ppermute | solution.py:439
  193.3 28.1 %collective-permute-start.29 = (bf16[32,64,256]{2,1,0:T(8,128)(2,1)S(1)}, bf16[32,64,256]{2,1,0:T(8,128)(2,1)S(1)}, u32[]{:S(2)}, u32[]{:S(2)}) collective-permute-start(bf16[32,64,256]{2,1,0:T(8,128)(2,1)S(1)} %add_convert_fusion), channel_id=1, source_target_pairs={{0,2},{1,3},{2,0},{3,1},{4,6},{5,7},{6,4},{7,5},{8,10},{9,11},{10,... | collective-permute-start | bytes 3145736 | tf_op jit(solution)/shard_map/ppermute | solution.py:439
  (36 other events, 292.3 us)
